TPU v7x, 256 devices: a whole 4x4x8 slice. The times are simulated.
256 devices in a mesh: seq: 16 (over y, x), ctx: 16 (over z, core).
Axes of the slice: x: 4, y: 4, z: 8, core: 2. Of those that a mesh axis runs over, the one named last changes fastest.
Arguments:
- queries: bfloat16 [32768, 20, 128], P(('seq', 'ctx')), parts along dimension 0, may hold values from -1.6953125 to 1.6953125
- keys: bfloat16 [32768, 20, 128], P(('seq', 'ctx')), parts along dimension 0, may hold values from -1.6953125 to 1.6953125
- values: bfloat16 [32768, 20, 128], P(('seq', 'ctx')), parts along dimension 0, may hold values from -6 to 6
- outputs: bfloat16 [32768, 20, 128], P(('seq', 'ctx')), parts along dimension 0, may hold values from -6 to 6
- grad_out: bfloat16 [32768, 20, 128], P(('seq', 'ctx')), parts along dimension 0, may hold values from -6 to 6
- log_norm: bfloat16 [32768, 20], P(('seq', 'ctx')), parts along dimension 0, as said below
- block_position: int32 [256], P('seq'), parts along dimension 0, may hold values from 0 to 15, as said below
Outputs:
- grad_queries: bfloat16 [32768, 20, 128], P(('seq', 'ctx')), parts along dimension 0
- grad_keys: bfloat16 [32768, 20, 128], P(('seq', 'ctx')), parts along dimension 0
- grad_values: bfloat16 [32768, 20, 128], P(('seq', 'ctx')), parts along dimension 0
There are 16 independent parts, one for each index of `seq`. A program takes and returns all parts, laid end to end along the dimension named above; each array names one. Nothing has to cross between parts.
Inputs may be any that keep to these rules, and one draw needn't show every extreme that they name: `block_position`: a permutation of the block numbers. log_norm[r, h] lies between log(p + 1) + 0.2 and log(p + 1) + 1.2 before rounding to bfloat16, with p = position[r].
All inputs are finite; a program needn't handle non-finite values.
Results may differ from a plain program's by a relative error of at most 0.0095.
Values may be sent and summed in bfloat16 or wider, within the bound.
A program may use at most 128 MiB of HBM per device.

v0:
```python
import math

import jax
import jax.numpy as jnp
from jax import lax
from jax.sharding import PartitionSpec as P


def logical_rows(first_row, piece_rows, block_rows, block_position):
    global_rows = first_row + jnp.arange(piece_rows, dtype=jnp.int32)
    owners = global_rows // block_rows
    owner_match = owners[:, None] == jnp.arange(block_position.shape[0], dtype=jnp.int32)[None, :]
    blocks = jnp.sum(jnp.where(owner_match, block_position[None, :], 0), axis=1)
    return blocks * block_rows + global_rows % block_rows


def body(queries, keys, values, outputs, grad_out, log_norm, block_position):
    group_size = lax.axis_size("ctx")
    device = lax.axis_index("ctx")
    block_rows, head_count, head_width = queries.shape
    score_scale = 1.0 / math.sqrt(head_width)
    key_place = logical_rows(device * block_rows, block_rows, block_rows, block_position)
    key_base = jnp.min(key_place)
    row_delta = jnp.einsum(
        "qhc,qhc->qh", grad_out, outputs, preferred_element_type=jnp.float32
    ).astype(jnp.bfloat16)
    zero_grads = jnp.zeros((block_rows, head_count, head_width), jnp.float32)
    stored_init = jnp.zeros((block_rows * group_size, head_count, head_width), jnp.bfloat16)
    initial = (zero_grads, zero_grads, stored_init)
    query_rows = lax.all_gather(queries, "ctx", axis=0, tiled=True)
    grad_rows = lax.all_gather(grad_out, "ctx", axis=0, tiled=True)
    norm_rows = lax.all_gather(log_norm, "ctx", axis=0, tiled=True)
    delta_rows = lax.all_gather(row_delta, "ctx", axis=0, tiled=True)
    piece_rows = query_rows.shape[0]
    positions = logical_rows(jnp.int32(0), piece_rows, block_rows, block_position)

    def compute(state):
        scores = (
            jnp.einsum("qhc,khc->hqk", query_rows, keys, preferred_element_type=jnp.float32)
            * score_scale
        )
        visible = key_place[None, None, :] <= positions[None, :, None]
        norm_f32 = norm_rows.astype(jnp.float32).T
        attn_weights = jnp.where(visible, jnp.exp(scores - norm_f32[:, :, None]), 0.0)
        grad_weights = jnp.einsum(
            "qhc,khc->hqk", grad_rows, values, preferred_element_type=jnp.float32
        )
        delta_f32 = delta_rows.astype(jnp.float32).T
        grad_scores = (attn_weights * (grad_weights - delta_f32[:, :, None])).astype(jnp.bfloat16)
        weights_low = attn_weights.astype(jnp.bfloat16)
        value_sum = jnp.einsum(
            "hqk,qhc->khc", weights_low, grad_rows, preferred_element_type=jnp.float32
        )
        key_sum = jnp.einsum(
            "hqk,qhc->khc", grad_scores, query_rows, preferred_element_type=jnp.float32
        )
        dq_part = jnp.einsum(
            "hqk,khc->qhc", grad_scores, keys, preferred_element_type=jnp.float32
        ).astype(jnp.bfloat16)
        return (key_sum, value_sum, dq_part)

    def unchanged(state):
        return state

    running = lax.cond(jnp.max(positions) >= key_base, compute, unchanged, initial)
    key_sum, value_sum, stored = running
    grad_keys = (key_sum * score_scale).astype(jnp.bfloat16)
    grad_values = value_sum.astype(jnp.bfloat16)
    shaped = stored.reshape(group_size, block_rows, head_count, head_width)
    received = lax.all_to_all(shaped, "ctx", split_axis=0, concat_axis=0, tiled=True)
    summed = jnp.sum(received.astype(jnp.float32), axis=0)
    grad_queries = (summed * score_scale).astype(jnp.bfloat16)
    return (grad_queries, grad_keys, grad_values)


def solution(mesh):
    in_specs = (
        P(("seq", "ctx"), None, None),
        P(("seq", "ctx"), None, None),
        P(("seq", "ctx"), None, None),
        P(("seq", "ctx"), None, None),
        P(("seq", "ctx"), None, None),
        P(("seq", "ctx"), None),
        P("seq"),
    )
    out_specs = (
        P(("seq", "ctx"), None, None),
        P(("seq", "ctx"), None, None),
        P(("seq", "ctx"), None, None),
    )
    return jax.shard_map(body, mesh=mesh, in_specs=in_specs, out_specs=out_specs, check_vma=False)
```

profile of v0, /device:TPU:1, one launch (start us, length us, event | category | flops | bytes accessed | tf_op | source)
XLA Modules:
  0.0 461.4 jit_solution(6120446191335304964)
XLA Ops:
  7.2 0.0 all-gather.3.cloned.1.call-start
  7.2 0.7 all-gather.3.cloned.1.call-update
  7.9 0.0 all-gather.5.cloned.1.call-start
  7.9 0.7 all-gather.5.cloned.1.call-update
  8.7 0.7 select_reduce_fusion.1
  9.4 0.8 select_reduce_fusion
  10.2 0.6 fusion.25
  10.8 0.6 fusion.27
  12.8 1.7 fusion.15
  14.5 21.8 %all_gather.15 = bf16[2048,20]{0,1:T(8,128)(2,1)S(1)} all-gather(bf16[128,20]{0,1:T(8,128)(2,1)S(1)} %fusion.15), channel_id=1, replica_groups=mesh['seq'=16,'ctx'=16] {'ctx'}, dimensions={0}, use_global_device_ids=true | all-gather | bytes 87040 | tf_op jit(solution)/shard_map/all_gather | solution.py:33
  36.2 15.3 %all_gather.13 = bf16[2048,20]{0,1:T(8,128)(2,1)S(1)} all-gather(bf16[128,20]{0,1:T(8,128)(2,1)} %param.14), channel_id=1, replica_groups=mesh['seq'=16,'ctx'=16] {'ctx'}, dimensions={0}, use_global_device_ids=true | all-gather | bytes 87040 | tf_op jit(solution)/shard_map/all_gather | solution.py:32
  51.5 29.2 %all-gather.3.cloned.1.call-done = bf16[2048,20,128]{2,0,1:T(8,128)(2,1)} async-done(((bf16[128,20,128]{2,0,1:T(8,128)(2,1)}), bf16[2048,20,128]{2,0,1:T(8,128)(2,1)}) %all-gather.3.cloned.1.call-update) | async-done | bytes 10485776 | tf_op jit(solution)/shard_map/all_gather | solution.py:30
  80.7 66.1 %all-gather.5.cloned.1.call-done = bf16[2048,20,128]{2,0,1:T(8,128)(2,1)} async-done(((bf16[128,20,128]{2,0,1:T(8,128)(2,1)}), bf16[2048,20,128]{2,0,1:T(8,128)(2,1)}) %all-gather.5.cloned.1.call-update) | async-done | bytes 10485776 | tf_op jit(solution)/shard_map/all_gather | solution.py:31
  146.8 53.8 %conditional.1 = (f32[128,20,128]{2,0,1:T(8,128)S(1)}, bf16[2048,20,128]{2,0,1:T(8,128)(2,1)}, bf16[128,20,128]{2,0,1:T(8,128)(2,1)S(1)}) conditional(s32[]{:T(128)} %convert_element_type.38, () %tuple.18, (s32[128]{0:T(128)S(1)}, s32[2048]{0:T(1024)S(1)}, bf16[2048,20,128]{2,0,1:T(8,128)(2,1)}, bf16[128,20,128]{2,0,1:T(8,128)(2,1)}, ...), branch_computations={%region_4.5_spmd, %region_5.6_spmd} | conditional | flops 6769229824 | bytes 157753952 | solution.py:65
  146.8 0.3 broadcast_compare_fusion
  147.2 5.8 %fusion.29 = f32[20,2048,128]{2,1,0:T(8,128)S(1)} fusion(bf16[2048,20,128]{2,0,1:T(8,128)(2,1)} %get-tuple-element.19, bf16[128,20,128]{2,0,1:T(8,128)(2,1)} %get-tuple-element.36), kind=kOutput, calls=%fused_computation.47 | convolution fusion | flops 1342177280 | bytes 32112640 | tf_op jit(solution)/shard_map/cond/branch_1_fun/qhc,khc->hqk/dot_general | solution.py:39
  153.0 0.0 copy-start.2
  153.0 14.2 %fusion.10 = bf16[128,20,128]{2,0,1:T(8,128)(2,1)S(1)} fusion(bf16[2048,20,128]{2,0,1:T(8,128)(2,1)} %get-tuple-element.22, f32[20,2048,128]{2,1,0:T(8,128)S(1)} %fusion.29, f32[20,2048]{1,0:T(8,128)S(1)} %get-tuple-element.43, pred[2048,128]{1,0:T(8,128)(4,1)S(1)} %broadcast_compare_fusion), kind=kOutput, calls=%fused_computation.11 | convolution fusion | flops 1363476480 | bytes 32538624 | tf_op jit(solution)/shard_map/cond/branch_1_fun/hqk,qhc->khc/dot_general | solution.py:51
  167.2 0.0 copy-done.2
  167.2 15.5 %multiply_convert_fusion = bf16[20,2048,128]{2,1,0:T(8,128)(2,1)} fusion(f32[20,2048,128]{2,1,0:T(8,128)S(1)} %fusion.29, f32[20,2048]{1,0:T(8,128)S(1)} %get-tuple-element.42, f32[20,2048]{1,0:T(8,128)S(1)} %get-tuple-element.43, pred[2048,128]{1,0:T(8,128)(4,1)S(1)} %broadcast_compare_fusion, bf16[2048,20,128]{2,0,1:T(8,128)(2,1)} %get-tuple-element.22, ...), kind=kOutput, calls=%fused_computation | convolution fusion | flops 1373634560 | bytes 43188224 | tf_op jit(solution)/shard_map/cond/branch_1_fun/qhc,khc->hqk/dot_general | solution.py:45
  182.7 0.0 copy-start
  182.7 10.1 %convolution_bitcast_fusion = f32[128,20,128]{2,0,1:T(8,128)S(1)} fusion(bf16[20,2048,128]{2,1,0:T(8,128)(2,1)} %multiply_convert_fusion, bf16[2048,20,128]{2,0,1:T(8,128)(2,1)} %get-tuple-element.19), kind=kOutput, calls=%fused_computation.9 | convolution fusion | flops 1342177280 | bytes 22282240 | tf_op jit(solution)/shard_map/cond/branch_1_fun/hqk,qhc->khc/dot_general | solution.py:54
  192.8 0.0 copy-done
  192.8 7.8 %convert_bitcast_fusion = bf16[2048,20,128]{2,0,1:T(8,128)(2,1)} fusion(bf16[20,2048,128]{2,1,0:T(8,128)(2,1)} %multiply_convert_fusion, bf16[128,20,128]{2,0,1:T(8,128)(2,1)S(1)} %copy-done), kind=kOutput, calls=%fused_computation.4 | convolution fusion | flops 1347420160 | bytes 21626880 | tf_op jit(solution)/shard_map/cond/branch_1_fun/hqk,khc->qhc/dot_general | solution.py:57
  200.6 0.0 copy-start.1
  200.6 13.0 %copy.21 = bf16[16,128,20,128]{3,1,2,0:T(8,128)(2,1)} copy(bf16[16,128,20,128]{3,1,0,2:T(8,128)(2,1)} %bitcast.5) | data formatting | bytes 20971520 | tf_op jit(solution)/shard_map/reshape | solution.py:69
  213.7 0.0 copy-done.1
  213.7 4.8 %all-to-all-start = ((bf16[16,128,20,128]{3,1,2,0:T(8,128)(2,1)}), bf16[16,128,20,128]{3,1,2,0:T(8,128)(2,1)}, u32[]{:S(2)}, u32[]{:S(2)}) async-start(bf16[16,128,20,128]{3,1,2,0:T(8,128)(2,1)} %copy.21), calls=%async_computation | async-start | bytes 20971520 | tf_op jit(solution)/shard_map/all_to_all | solution.py:70
  218.5 1.0 multiply_convert_fusion.1
  219.5 227.5 %all-to-all-done = bf16[16,128,20,128]{3,1,2,0:T(8,128)(2,1)} async-done(((bf16[16,128,20,128]{3,1,2,0:T(8,128)(2,1)}), bf16[16,128,20,128]{3,1,2,0:T(8,128)(2,1)}, u32[]{:S(2)}, u32[]{:S(2)}) %all-to-all-start) | async-done | bytes 10485792 | tf_op jit(solution)/shard_map/all_to_all | solution.py:70
  447.1 6.5 %convert_reduce_fusion = f32[128,20,128]{2,0,1:T(8,128)S(1)} fusion(bf16[16,128,20,128]{3,1,2,0:T(8,128)(2,1)} %all-to-all-done), kind=kLoop, calls=%fused_computation.17 | loop fusion | flops 10158080 | bytes 11796480 | tf_op jit(solution)/shard_map/reduce_sum | solution.py:71
  453.6 1.0 multiply_convert_fusion.2
  (3 shorter events, 0.0 us)
Async XLA Ops:
  7.2 73.5 %all-gather.3.cloned.1.call-start = ((), (), s32[]{:S(2)}) async-start(), calls=%async_computation.1 | async-start | bytes 11141120 | tf_op jit(solution)/shard_map/all_gather | solution.py:30
  7.9 138.9 %all-gather.5.cloned.1.call-start = ((), (), s32[]{:S(2)}) async-start(), calls=%async_computation.2 | async-start | bytes 11141120 | tf_op jit(solution)/shard_map/all_gather | solution.py:31
  153.0 14.2 %copy-start.2 = (bf16[128,20,128]{2,0,1:T(8,128)(2,1)S(1)}, bf16[128,20,128]{2,0,1:T(8,128)(2,1)}, u32[]{:S(2)}) copy-start(bf16[128,20,128]{2,0,1:T(8,128)(2,1)} %get-tuple-element.37) | copy-start | bytes 1966084 | tf_op jit(solution)/shard_map/cond
  182.7 10.1 %copy-start = (bf16[128,20,128]{2,0,1:T(8,128)(2,1)S(1)}, bf16[128,20,128]{2,0,1:T(8,128)(2,1)}, u32[]{:S(2)}) copy-start(bf16[128,20,128]{2,0,1:T(8,128)(2,1)} %get-tuple-element.36) | copy-start | bytes 1966084 | tf_op jit(solution)/shard_map/cond
  200.6 13.0 %copy-start.1 = (bf16[128,20,128]{2,0,1:T(8,128)(2,1)}, bf16[128,20,128]{2,0,1:T(8,128)(2,1)S(1)}, u32[]{:S(2)}) copy-start(bf16[128,20,128]{2,0,1:T(8,128)(2,1)S(1)} %get-tuple-element.30) | copy-start | bytes 1966084
  213.7 233.4 %all-to-all-start = ((bf16[16,128,20,128]{3,1,2,0:T(8,128)(2,1)}), bf16[16,128,20,128]{3,1,2,0:T(8,128)(2,1)}, u32[]{:S(2)}, u32[]{:S(2)}) async-start(bf16[16,128,20,128]{3,1,2,0:T(8,128)(2,1)} %copy.21), calls=%async_computation | async-start | bytes 20971520 | tf_op jit(solution)/shard_map/all_to_all | solution.py:70
Sparse Core Ops, SparseCore 0:
  9.8 70.7 all-gather.2
  82.5 64.2 all-gather.4
where the time goes:
time: 462 us; the launch traced here: 461 us
  waiting for transfers between devices  324 us (70%)
  matrix products  53.4 us (12%)
  blocking collectives  37.1 us (8%)
  between operations  15.4 us (3%)
  other arithmetic  13.4 us (3%)
  local copies, waits for them, and re-layouts  13 us (3%)
  starting transfers between devices  4.92 us (1%)
    all_to_all x1, waiting for transfers between devices, body(): lax.all_to_all(shaped, 'ctx', split_axis=0, concat_axis=0, tiled=True)  228 us
    all_gather x1, waiting for transfers between devices, body(): grad_rows = lax.all_gather(grad_out, 'ctx', axis=0, tiled=True)  66.1 us
    all_gather x1, waiting for transfers between devices, body(): query_rows = lax.all_gather(queries, 'ctx', axis=0, tiled=True)  29.2 us
    all_gather x1, blocking collectives, body(): delta_rows = lax.all_gather(row_delta, 'ctx', axis=0, tiled=True)  21.8 us
    dot_general x1, matrix products, compute(): jnp.einsum('qhc,khc->hqk', grad_rows, values, preferred_element_type=jnp....  15.5 us
    all_gather x1, blocking collectives, body(): norm_rows = lax.all_gather(log_norm, 'ctx', axis=0, tiled=True)  15.3 us
    dot_general x1, matrix products, compute(): jnp.einsum('hqk,qhc->khc', weights_low, grad_rows, preferred_element_type...  14.2 us
    reshape x1, local copies, waits for them, and re-layouts, body(): shaped = stored.reshape(group_size, block_rows, head_count, head_width)  13 us
  transfers between devices with their start and end apart: 3, of which 3 were waited for; matrix products, arithmetic and copies ran while one was open for 1% of the time, Pallas kernels for 0%

commit v1 on v0

v1 whole, which is shorter than its diff:
```python
import math

import jax
import jax.numpy as jnp
from jax import lax
from jax.experimental import pallas as pl
from jax.experimental.pallas import tpu as pltpu
from jax.sharding import PartitionSpec as P

N = 16
ROWS = 128
WIDTH = 128
HEADS = 20
EXTRA = HEADS - N
STRIDE = N // EXTRA
CHIPS = N // 2
PAIR = 2 * ROWS
LOG2E = math.log2(math.e)
SCALE = 1.0 / math.sqrt(WIDTH)
HIDE = 1e30
K, V, Q, G, AUX = range(5)
DQ, DK, DV = range(3)


def swing(step):
    return (step + 1) // 2 * (2 * (step % 2) - 1)


def mm(a, b):
    return lax.dot_general(a, b, (((1,), (0,)), ((), ())), preferred_element_type=jnp.float32)


def mm_nt(a, b):
    return lax.dot_general(a, b, (((1,), (1,)), ((), ())), preferred_element_type=jnp.float32)


def kernel(
    q_ref, k_ref, v_ref, o_ref, g_ref, ln_ref, pos_ref,
    dq_ref, dk_ref, dv_ref,
    kb, vb, qb, gb, auxb, ov, gv, auxs, kt, dka, dva, dqo, dko, dvo,
    load_sem, in_send, in_recv, out_send, out_recv,
):
    me = lax.axis_index("ctx")
    chip = me // 2
    two = me % STRIDE == 0
    extra_head = N + me // STRIDE
    sources = (k_ref, v_ref, q_ref, g_ref, auxs)
    landing = (kb, vb, qb, gb, auxb)
    staged = (dqo, dko, dvo)
    results = (dq_ref, dk_ref, dv_ref)

    def wait(ref, sem):
        pltpu.make_async_copy(ref, ref, sem).wait()

    def send(kind, head, slot, dest):
        pltpu.make_async_remote_copy(
            src_ref=sources[kind].at[head],
            dst_ref=landing[kind].at[slot, me],
            send_sem=in_send.at[kind, head],
            recv_sem=in_recv.at[kind, slot, me],
            device_id={"ctx": dest},
            device_id_type=pl.DeviceIdType.MESH,
        ).start()

    def keep(kind, head, slot):
        pltpu.make_async_copy(
            sources[kind].at[head], landing[kind].at[slot, me], in_recv.at[kind, slot, me]
        ).start()

    def send_extra(kinds):
        def one(i, carry):
            which = (me // STRIDE + i) % EXTRA
            dest = which * STRIDE

            @pl.when(dest != me)
            def _():
                for kind in kinds:
                    send(kind, N + which, 0, dest)

            @pl.when(dest == me)
            def _():
                for kind in kinds:
                    keep(kind, N + which, 0)

            return carry

        lax.fori_loop(0, EXTRA, one, 0)

    def send_main(kinds):
        for kind in kinds:
            keep(kind, me, 1)

        def one(i, carry):
            dest = (me + swing(i) + N) % N
            for kind in kinds:
                send(kind, dest, 1, dest)
            return carry

        lax.fori_loop(1, N, one, 0)

    load_g = pltpu.make_async_copy(g_ref, gv, load_sem.at[0])
    load_o = pltpu.make_async_copy(o_ref, ov, load_sem.at[1])
    load_g.start()
    load_o.start()
    barrier = pltpu.get_barrier_semaphore()

    def greet(i, carry):
        pl.semaphore_signal(
            barrier, inc=1, device_id={"ctx": (me + i) % N}, device_id_type=pl.DeviceIdType.MESH
        )
        return carry

    lax.fori_loop(1, N, greet, 0)
    pl.semaphore_wait(barrier, N - 1)

    send_extra((K, V, Q, G))

    load_g.wait()
    load_o.wait()
    norm = ln_ref[...].astype(jnp.float32) * LOG2E
    ones = jnp.ones((8, WIDTH), jnp.bfloat16)
    upper = lax.broadcasted_iota(jnp.int32, (8, ROWS), 0) < 4
    for h in range(HEADS):
        product = gv[h].astype(jnp.float32) * ov[h].astype(jnp.float32)
        high = product.astype(jnp.bfloat16)
        low = (product - high.astype(jnp.float32)).astype(jnp.bfloat16)
        delta = (mm_nt(ones, high) + mm_nt(ones, low)).astype(jnp.bfloat16).astype(jnp.float32)
        auxs[h] = jnp.where(upper, norm[h : h + 1, :], delta)
    send_extra((AUX,))
    send_main((AUX,))
    send_main((K, V))
    send_main((Q, G))

    rows_k = lax.broadcasted_iota(jnp.int32, (ROWS, ROWS), 0)
    rows_q = lax.broadcasted_iota(jnp.int32, (ROWS, ROWS), 1)

    def one_pair(step, carry):
        slot = step // CHIPS
        turn = step % CHIPS
        head = jnp.where(slot == 0, extra_head, me)

        @pl.when(turn == 0)
        def _():
            dka[...] = jnp.zeros_like(dka)
            dva[...] = jnp.zeros_like(dva)

            def arrived(i, c):
                for kind in (K, V):
                    wait(landing[kind].at[slot, i], in_recv.at[kind, slot, i])
                return c

            lax.fori_loop(0, N, arrived, 0)
            for t in range(CHIPS):
                kt[t] = kb[slot, 2 * t : 2 * t + 2].reshape(PAIR, WIDTH).T

        c = (chip + swing(turn) + CHIPS) % CHIPS
        for b in range(2):
            for kind in (AUX, Q, G):
                wait(landing[kind].at[slot, 2 * c + b], in_recv.at[kind, slot, 2 * c + b])
        pair = pl.ds(2 * c, 2)
        queries = qb[slot, pair].reshape(PAIR, WIDTH)
        grads = gb[slot, pair].reshape(PAIR, WIDTH)
        queries_t = queries.T
        grads_t = grads.T
        norms = [auxb[slot, 2 * c + b, 0:1, :] for b in range(2)]
        delta = jnp.concatenate([auxb[slot, 2 * c + b, 4:5, :] for b in range(2)], axis=1)
        dq_t = jnp.zeros((WIDTH, PAIR), jnp.float32)
        for t in range(CHIPS):
            tile = (c + t) % CHIPS
            spot = pl.ds(2 * tile, 2)
            keys = kb[slot, spot].reshape(PAIR, WIDTH)
            vals = vb[slot, spot].reshape(PAIR, WIDTH)
            scores = mm(keys, queries_t) * (SCALE * LOG2E)
            grad_weights = mm(vals, grads_t)
            parts = []
            for kblock in range(2):
                bias = []
                for qblock in range(2):
                    later = pos_ref[2 * tile + kblock] > pos_ref[2 * c + qblock]
                    row = norms[qblock] + jnp.where(later, HIDE, 0.0)
                    if t == 0:
                        if kblock == qblock:
                            row = row + jnp.where(rows_k > rows_q, HIDE, 0.0)
                        else:
                            row = jnp.broadcast_to(row, (ROWS, ROWS))
                    bias.append(row)
                parts.append(
                    jnp.exp2(
                        scores[kblock * ROWS : (kblock + 1) * ROWS] - jnp.concatenate(bias, axis=1)
                    )
                )
            weights = jnp.concatenate(parts, axis=0)
            grad_scores = (weights * (grad_weights - delta)).astype(jnp.bfloat16)
            dva[tile] += mm(weights.astype(jnp.bfloat16), grads)
            dka[tile] += mm(grad_scores, queries)
            dq_t += mm(kt[tile], grad_scores)
        dqo[slot, pair] = (dq_t * SCALE).T.astype(jnp.bfloat16).reshape(2, ROWS, WIDTH)

        def give(kind, dest):
            src = staged[kind].at[slot, dest]
            dst = results[kind].at[head]

            @pl.when(dest != me)
            def _():
                pltpu.make_async_remote_copy(
                    src_ref=src,
                    dst_ref=dst,
                    send_sem=out_send.at[kind, slot, dest],
                    recv_sem=out_recv.at[kind, head],
                    device_id={"ctx": dest},
                    device_id_type=pl.DeviceIdType.MESH,
                ).start()

            @pl.when(dest == me)
            def _():
                pltpu.make_async_copy(src, dst, out_recv.at[kind, head]).start()

        for b in range(2):
            give(DQ, 2 * c + b)

        @pl.when(turn == CHIPS - 1)
        def _():
            def finish(i, carry):
                spot_chip = (chip + swing(i) + CHIPS) % CHIPS
                spot = pl.ds(2 * spot_chip, 2)
                dko[slot, spot] = (dka[spot_chip] * SCALE).astype(jnp.bfloat16).reshape(2, ROWS, WIDTH)
                dvo[slot, spot] = dva[spot_chip].astype(jnp.bfloat16).reshape(2, ROWS, WIDTH)
                for b in range(2):
                    give(DK, 2 * spot_chip + b)
                    give(DV, 2 * spot_chip + b)
                return carry

            lax.fori_loop(0, CHIPS, finish, 0)

        return carry

    lax.fori_loop(jnp.where(two, 0, CHIPS), 2 * CHIPS, one_pair, 0)

    def drain_in(h, carry):
        owner = jnp.where(h < N, h, (h - N) * STRIDE)

        @pl.when(owner != me)
        def _():
            for kind in range(5):
                wait(sources[kind].at[h], in_send.at[kind, h])

        return carry

    lax.fori_loop(0, HEADS, drain_in, 0)

    def drain_out(step, carry):
        slot = step // N
        dest = step % N

        @pl.when(dest != me)
        def _():
            for kind in range(3):
                wait(staged[kind].at[slot, dest], out_send.at[kind, slot, dest])

        return carry

    lax.fori_loop(jnp.where(two, 0, N), 2 * N, drain_out, 0)

    def collect(h, carry):
        for kind in range(3):
            wait(results[kind].at[h], out_recv.at[kind, h])
        return carry

    lax.fori_loop(0, HEADS, collect, 0)


def body(queries, keys, values, outputs, grad_out, log_norm, block_position):
    by_head = [jnp.transpose(x, (1, 0, 2)) for x in (queries, keys, values, outputs, grad_out)]
    whole = jax.ShapeDtypeStruct((HEADS, ROWS, WIDTH), jnp.bfloat16)
    blocks = pltpu.VMEM((2, N, ROWS, WIDTH), jnp.bfloat16)
    totals = pltpu.VMEM((CHIPS, PAIR, WIDTH), jnp.float32)
    results = pl.pallas_call(
        kernel,
        out_shape=(whole, whole, whole),
        in_specs=[pl.BlockSpec(memory_space=pl.ANY)] * 5
        + [pl.BlockSpec(memory_space=pltpu.VMEM), pl.BlockSpec(memory_space=pltpu.SMEM)],
        out_specs=[pl.BlockSpec(memory_space=pl.ANY)] * 3,
        scratch_shapes=[
            blocks, blocks, blocks, blocks,
            pltpu.VMEM((2, N, 8, ROWS), jnp.float32),
            pltpu.VMEM((HEADS, ROWS, WIDTH), jnp.bfloat16),
            pltpu.VMEM((HEADS, ROWS, WIDTH), jnp.bfloat16),
            pltpu.VMEM((HEADS, 8, ROWS), jnp.float32),
            pltpu.VMEM((CHIPS, WIDTH, PAIR), jnp.bfloat16),
            totals, totals,
            blocks, blocks, blocks,
            pltpu.SemaphoreType.DMA((2,)),
            pltpu.SemaphoreType.DMA((5, HEADS)),
            pltpu.SemaphoreType.DMA((5, 2, N)),
            pltpu.SemaphoreType.DMA((3, 2, N)),
            pltpu.SemaphoreType.DMA((3, HEADS)),
        ],
        compiler_params=pltpu.CompilerParams(
            collective_id=0, has_side_effects=True, vmem_limit_bytes=48 * 1024 * 1024
        ),
        name="attention_backward",
    )(*by_head, log_norm.T, block_position)
    return tuple(jnp.transpose(x, (1, 0, 2)) for x in results)


def solution(mesh):
    rows = P(("seq", "ctx"), None, None)
    return jax.shard_map(
        body,
        mesh=mesh,
        in_specs=(rows, rows, rows, rows, rows, P(("seq", "ctx"), None), P("seq")),
        out_specs=(rows, rows, rows),
        check_vma=False,
    )
```

time: 462 us -> 129 us (0.28)
  waiting for transfers between devices: 324 us -> 0 us
  Pallas kernels: 0 us -> 120 us
  matrix products: 53.4 us -> 0 us
  blocking collectives: 37.1 us -> 0 us
  between operations: 15.4 us -> 0.66 us
  other arithmetic: 13.4 us -> 0 us
  starting transfers between devices: 4.92 us -> 0 us
    all_to_all x1 -> x0, waiting for transfers between devices: 228 us -> none  [body(): lax.all_to_all(shaped, 'ctx', split_axis=0, concat_axis=0, tiled=True)]
    pallas_call x0 -> x1, Pallas kernels: none -> 120 us  [body(): pl.pallas_call(kernel, out_shape=(whole, whole, whole), in_specs=[pl.Bloc...]
    all_gather x2 -> x0, waiting for transfers between devices: 95.3 us -> none  [the longest x1 66.1 us: body(): grad_rows = lax.all_gather(grad_out, 'ctx', axis=0, tiled=True)]
    dot_general x5 -> x0, matrix products: 53.4 us -> none  [the longest x1 15.5 us: compute(): jnp.einsum('qhc,khc->hqk', grad_rows, values, preferred_element_type=jnp....]
    all_gather x2 -> x0, blocking collectives: 37.1 us -> none  [the longest x1 21.8 us: body(): delta_rows = lax.all_gather(row_delta, 'ctx', axis=0, tiled=True)]
    reshape x1 -> x0, local copies, waits for them, and re-layouts: 13 us -> none  [body(): shaped = stored.reshape(group_size, block_rows, head_count, head_width)]
    unnamed x2 -> x17, local copies, waits for them, and re-layouts: 0.01 us -> 8.62 us
    reduce_sum x3 -> x0, other arithmetic: 8.01 us -> none  [the longest x1 6.52 us: body(): summed = jnp.sum(received.astype(jnp.float32), axis=0)]
  transfers between devices with their start and end apart: 3 -> 0, of which waited for: 3 -> 0; matrix products, arithmetic and copies ran while one was open for 1% -> 0% of each run, Pallas kernels for 0% -> 0%
where the time goes in v1:
time: 129 us
  Pallas kernels  120 us (93%)
  local copies, waits for them, and re-layouts  8.62 us (7%)
    pallas_call x1, Pallas kernels, body(): pl.pallas_call(kernel, out_shape=(whole, whole, whole), in_specs=[pl.Bloc...  120 us
    unnamed x17, local copies, waits for them, and re-layouts  8.62 us

profile of v1, /device:TPU:1, one launch (start us, length us, event | category | flops | bytes accessed | tf_op | source)
XLA Modules:
  0.0 128.9 jit_solution(5244555328425104849)
XLA Ops:
  0.6 0.0 copy-start.5
  0.6 0.0 copy-start.6
  0.7 0.7 copy-done.5
  1.3 0.0 copy-done.6
  1.3 0.0 copy-start
  1.3 1.1 copy-done
  2.4 0.0 copy-start.1
  2.4 1.1 copy-done.1
  3.5 0.0 copy-start.2
  3.5 1.1 copy-done.2
  4.6 0.0 copy-start.3
  4.6 1.1 copy-done.3
  5.7 0.0 copy-start.4
  5.7 1.1 copy-done.4
  6.8 119.6 %attention_backward.1 = (bf16[20,128,128]{2,1,0:T(8,128)(2,1)S(1)}, bf16[20,128,128]{2,1,0:T(8,128)(2,1)S(1)}, bf16[20,128,128]{2,1,0:T(8,128)(2,1)S(1)}) custom-call(bf16[20,128,128]{2,1,0:T(8,128)(2,1)S(1)} %bitcast.12, bf16[20,128,128]{2,1,0:T(8,128)(2,1)S(1)} %bitcast.13, bf16[20,128,128]{2,1,0:T(8,128)(2,1)S(1)} %bitcast.14, ...), custom_call_target="tpu_custom_call" | custom-call | tf_op jit(solution)/shard_map/attention_backward/pallas_call | solution.py:277
  126.4 0.8 copy.13
  127.2 0.8 copy.14
  128.1 0.8 copy.15
Async XLA Ops:
  0.6 0.7 copy-start.5
  0.6 0.7 copy-start.6
  1.3 1.1 copy-start
  2.4 1.1 copy-start.1
  3.5 1.1 copy-start.2
  4.6 1.1 copy-start.3
  5.7 1.1 copy-start.4

commit v2 on v1

--- a/solution.py
+++ b/solution.py
@@ -37,7 +37,7 @@
 def kernel(
     q_ref, k_ref, v_ref, o_ref, g_ref, ln_ref, pos_ref,
     dq_ref, dk_ref, dv_ref,
-    kb, vb, qb, gb, auxb, ov, gv, auxs, kt, dka, dva, dqo, dko, dvo,
+    kb, vb, qb, gb, auxb, ov, gv, auxs, qt, gt, tri, dqa, dqo, dko, dvo,
     load_sem, in_send, in_recv, out_send, out_recv,
 ):
     me = lax.axis_index("ctx")
@@ -113,7 +113,7 @@
     lax.fori_loop(1, N, greet, 0)
     pl.semaphore_wait(barrier, N - 1)
 
-    send_extra((K, V, Q, G))
+    send_extra((Q, G))
 
     load_g.wait()
     load_o.wait()
@@ -128,73 +128,20 @@
         auxs[h] = jnp.where(upper, norm[h : h + 1, :], delta)
     send_extra((AUX,))
     send_main((AUX,))
+    send_extra((K, V))
+    send_main((Q, G))
     send_main((K, V))
-    send_main((Q, G))
-
-    rows_k = lax.broadcasted_iota(jnp.int32, (ROWS, ROWS), 0)
-    rows_q = lax.broadcasted_iota(jnp.int32, (ROWS, ROWS), 1)
+
+    below = lax.broadcasted_iota(jnp.int32, (ROWS, ROWS), 0) > lax.broadcasted_iota(
+        jnp.int32, (ROWS, ROWS), 1
+    )
+    tri[0] = jnp.zeros((ROWS, ROWS), jnp.float32)
+    tri[1] = jnp.where(below, HIDE, 0.0)
 
     def one_pair(step, carry):
         slot = step // CHIPS
         turn = step % CHIPS
         head = jnp.where(slot == 0, extra_head, me)
-
-        @pl.when(turn == 0)
-        def _():
-            dka[...] = jnp.zeros_like(dka)
-            dva[...] = jnp.zeros_like(dva)
-
-            def arrived(i, c):
-                for kind in (K, V):
-                    wait(landing[kind].at[slot, i], in_recv.at[kind, slot, i])
-                return c
-
-            lax.fori_loop(0, N, arrived, 0)
-            for t in range(CHIPS):
-                kt[t] = kb[slot, 2 * t : 2 * t + 2].reshape(PAIR, WIDTH).T
-
-        c = (chip + swing(turn) + CHIPS) % CHIPS
-        for b in range(2):
-            for kind in (AUX, Q, G):
-                wait(landing[kind].at[slot, 2 * c + b], in_recv.at[kind, slot, 2 * c + b])
-        pair = pl.ds(2 * c, 2)
-        queries = qb[slot, pair].reshape(PAIR, WIDTH)
-        grads = gb[slot, pair].reshape(PAIR, WIDTH)
-        queries_t = queries.T
-        grads_t = grads.T
-        norms = [auxb[slot, 2 * c + b, 0:1, :] for b in range(2)]
-        delta = jnp.concatenate([auxb[slot, 2 * c + b, 4:5, :] for b in range(2)], axis=1)
-        dq_t = jnp.zeros((WIDTH, PAIR), jnp.float32)
-        for t in range(CHIPS):
-            tile = (c + t) % CHIPS
-            spot = pl.ds(2 * tile, 2)
-            keys = kb[slot, spot].reshape(PAIR, WIDTH)
-            vals = vb[slot, spot].reshape(PAIR, WIDTH)
-            scores = mm(keys, queries_t) * (SCALE * LOG2E)
-            grad_weights = mm(vals, grads_t)
-            parts = []
-            for kblock in range(2):
-                bias = []
-                for qblock in range(2):
-                    later = pos_ref[2 * tile + kblock] > pos_ref[2 * c + qblock]
-                    row = norms[qblock] + jnp.where(later, HIDE, 0.0)
-                    if t == 0:
-                        if kblock == qblock:
-                            row = row + jnp.where(rows_k > rows_q, HIDE, 0.0)
-                        else:
-                            row = jnp.broadcast_to(row, (ROWS, ROWS))
-                    bias.append(row)
-                parts.append(
-                    jnp.exp2(
-                        scores[kblock * ROWS : (kblock + 1) * ROWS] - jnp.concatenate(bias, axis=1)
-                    )
-                )
-            weights = jnp.concatenate(parts, axis=0)
-            grad_scores = (weights * (grad_weights - delta)).astype(jnp.bfloat16)
-            dva[tile] += mm(weights.astype(jnp.bfloat16), grads)
-            dka[tile] += mm(grad_scores, queries)
-            dq_t += mm(kt[tile], grad_scores)
-        dqo[slot, pair] = (dq_t * SCALE).T.astype(jnp.bfloat16).reshape(2, ROWS, WIDTH)
 
         def give(kind, dest):
             src = staged[kind].at[slot, dest]
@@ -215,19 +162,71 @@
             def _():
                 pltpu.make_async_copy(src, dst, out_recv.at[kind, head]).start()
 
+        def around(i):
+            return (chip + swing(i) + CHIPS) % CHIPS
+
+        @pl.when(turn == 0)
+        def _():
+            dqa[...] = jnp.zeros_like(dqa)
+
+            def arrived(i, carry):
+                c = around(i)
+                for b in range(2):
+                    for kind in (AUX, Q, G):
+                        wait(landing[kind].at[slot, 2 * c + b], in_recv.at[kind, slot, 2 * c + b])
+                qt[c] = qb[slot, pl.ds(2 * c, 2)].reshape(PAIR, WIDTH).T
+                gt[c] = gb[slot, pl.ds(2 * c, 2)].reshape(PAIR, WIDTH).T
+                return carry
+
+            lax.fori_loop(0, CHIPS, arrived, 0)
+
+        c = around(turn)
         for b in range(2):
-            give(DQ, 2 * c + b)
+            for kind in (K, V):
+                wait(landing[kind].at[slot, 2 * c + b], in_recv.at[kind, slot, 2 * c + b])
+        pair = pl.ds(2 * c, 2)
+        keys = kb[slot, pair].reshape(PAIR, WIDTH)
+        vals = vb[slot, pair].reshape(PAIR, WIDTH)
+        keys_t = keys.T
+        dk = jnp.zeros((PAIR, WIDTH), jnp.float32)
+        dv = jnp.zeros((PAIR, WIDTH), jnp.float32)
+        for t in range(CHIPS):
+            spot = slice(2 * t, 2 * t + 2)
+            queries = qb[slot, spot].reshape(PAIR, WIDTH)
+            grads = gb[slot, spot].reshape(PAIR, WIDTH)
+            norms = [auxb[slot, 2 * t + b, 0:1, :] for b in range(2)]
+            delta = jnp.concatenate([auxb[slot, 2 * t + b, 4:5, :] for b in range(2)], axis=1)
+            diagonal = tri[jnp.where(c == t, 1, 0)]
+            scores = mm(keys, qt[t]) * (SCALE * LOG2E)
+            grad_weights = mm(vals, gt[t])
+            parts = []
+            for kblock in range(2):
+                bias = []
+                for qblock in range(2):
+                    later = pos_ref[2 * c + kblock] > pos_ref[2 * t + qblock]
+                    row = norms[qblock] + jnp.where(later, HIDE, 0.0)
+                    bias.append(row + diagonal if kblock == qblock else jnp.broadcast_to(row, (ROWS, ROWS)))
+                part = scores[kblock * ROWS : (kblock + 1) * ROWS]
+                parts.append(jnp.exp2(part - jnp.concatenate(bias, axis=1)))
+            weights = jnp.concatenate(parts, axis=0)
+            grad_scores = (weights * (grad_weights - delta)).astype(jnp.bfloat16)
+            dv += mm(weights.astype(jnp.bfloat16), grads)
+            dk += mm(grad_scores, queries)
+            dqa[t] += mm(keys_t, grad_scores)
+        dko[slot, pair] = (dk * SCALE).astype(jnp.bfloat16).reshape(2, ROWS, WIDTH)
+        dvo[slot, pair] = dv.astype(jnp.bfloat16).reshape(2, ROWS, WIDTH)
+        for b in range(2):
+            give(DK, 2 * c + b)
+            give(DV, 2 * c + b)
 
         @pl.when(turn == CHIPS - 1)
         def _():
             def finish(i, carry):
-                spot_chip = (chip + swing(i) + CHIPS) % CHIPS
-                spot = pl.ds(2 * spot_chip, 2)
-                dko[slot, spot] = (dka[spot_chip] * SCALE).astype(jnp.bfloat16).reshape(2, ROWS, WIDTH)
-                dvo[slot, spot] = dva[spot_chip].astype(jnp.bfloat16).reshape(2, ROWS, WIDTH)
+                c = around(i)
+                done = (dqa[c] * SCALE).T.astype(jnp.bfloat16)
+                dqo[slot, pl.ds(2 * c, 2)] = done.reshape(2, ROWS, WIDTH)
                 for b in range(2):
-                    give(DK, 2 * spot_chip + b)
-                    give(DV, 2 * spot_chip + b)
+                    give(DQ, 2 * c + b)
                 return carry
 
             lax.fori_loop(0, CHIPS, finish, 0)
@@ -273,7 +272,6 @@
     by_head = [jnp.transpose(x, (1, 0, 2)) for x in (queries, keys, values, outputs, grad_out)]
     whole = jax.ShapeDtypeStruct((HEADS, ROWS, WIDTH), jnp.bfloat16)
     blocks = pltpu.VMEM((2, N, ROWS, WIDTH), jnp.bfloat16)
-    totals = pltpu.VMEM((CHIPS, PAIR, WIDTH), jnp.float32)
     results = pl.pallas_call(
         kernel,
         out_shape=(whole, whole, whole),
@@ -287,7 +285,9 @@
             pltpu.VMEM((HEADS, ROWS, WIDTH), jnp.bfloat16),
             pltpu.VMEM((HEADS, 8, ROWS), jnp.float32),
             pltpu.VMEM((CHIPS, WIDTH, PAIR), jnp.bfloat16),
-            totals, totals,
+            pltpu.VMEM((CHIPS, WIDTH, PAIR), jnp.bfloat16),
+            pltpu.VMEM((2, ROWS, ROWS), jnp.float32),
+            pltpu.VMEM((CHIPS, WIDTH, PAIR), jnp.float32),
             blocks, blocks, blocks,
             pltpu.SemaphoreType.DMA((2,)),
             pltpu.SemaphoreType.DMA((5, HEADS)),
@@ -296,7 +296,7 @@
             pltpu.SemaphoreType.DMA((3, HEADS)),
         ],
         compiler_params=pltpu.CompilerParams(
-            collective_id=0, has_side_effects=True, vmem_limit_bytes=48 * 1024 * 1024
+            collective_id=0, has_side_effects=True, vmem_limit_bytes=62 * 1024 * 1024
         ),
         name="attention_backward",
     )(*by_head, log_norm.T, block_position)

time: 129 us -> 124 us (0.961)
  local copies, waits for them, and re-layouts: 8.62 us -> 4.21 us
    unnamed x17 -> x7, local copies, waits for them, and re-layouts: 8.62 us -> 4.21 us
where the time goes in v2:
time: 124 us
  Pallas kernels  119 us (96%)
  local copies, waits for them, and re-layouts  4.21 us (3%)
    pallas_call x1, Pallas kernels, body(): pl.pallas_call(kernel, out_shape=(whole, whole, whole), in_specs=[pl.Bloc...  119 us
    unnamed x7, local copies, waits for them, and re-layouts  4.21 us

profile of v2, /device:TPU:1, one launch (start us, length us, event | category | flops | bytes accessed | tf_op | source)
XLA Modules:
  0.0 124.2 jit_solution(2411392314591487686)
XLA Ops:
  0.6 119.4 %attention_backward.1 = (bf16[20,128,128]{2,1,0:T(8,128)(2,1)}, bf16[20,128,128]{2,1,0:T(8,128)(2,1)}, bf16[20,128,128]{2,1,0:T(8,128)(2,1)}) custom-call(bf16[20,128,128]{2,1,0:T(8,128)(2,1)} %bitcast.12, bf16[20,128,128]{2,1,0:T(8,128)(2,1)} %bitcast.13, bf16[20,128,128]{2,1,0:T(8,128)(2,1)} %bitcast.14, bf16[20,128,128]{2,1,0:T(8,128)(2,1)} %bitcast.15, ...), custom_call_target="tpu_custom_call" | custom-call | tf_op jit(solution)/shard_map/attention_backward/pallas_call | solution.py:275
  120.0 0.0 copy-start.1
  120.0 2.0 %copy.13 = bf16[128,20,128]{2,0,1:T(8,128)(2,1)} copy(bf16[128,20,128]{2,0,1:T(8,128)(2,1)} %bitcast.11) | data formatting | bytes 1310720
  122.1 0.0 copy-done.1
  122.1 0.0 copy-start
  122.1 0.8 copy.14
  122.9 0.5 copy-done
  123.4 0.8 copy.15
Async XLA Ops:
  120.0 2.1 %copy-start.1 = (bf16[20,128,128]{2,1,0:T(8,128)(2,1)S(1)}, bf16[20,128,128]{2,1,0:T(8,128)(2,1)}, u32[]{:S(2)}) copy-start(bf16[20,128,128]{2,1,0:T(8,128)(2,1)} %get-tuple-element.7) | copy-start | bytes 1966084
  122.1 1.3 %copy-start = (bf16[20,128,128]{2,1,0:T(8,128)(2,1)S(1)}, bf16[20,128,128]{2,1,0:T(8,128)(2,1)}, u32[]{:S(2)}) copy-start(bf16[20,128,128]{2,1,0:T(8,128)(2,1)} %get-tuple-element.8) | copy-start | bytes 1966084

commit v3 on v2

--- a/solution.py
+++ b/solution.py
@@ -42,6 +42,7 @@
 ):
     me = lax.axis_index("ctx")
     chip = me // 2
+    sign = 1 - 2 * (me % 2)
     two = me % STRIDE == 0
     extra_head = N + me // STRIDE
     sources = (k_ref, v_ref, q_ref, g_ref, auxs)
@@ -91,7 +92,7 @@
             keep(kind, me, 1)
 
         def one(i, carry):
-            dest = (me + swing(i) + N) % N
+            dest = (me + sign * swing(i) + N) % N
             for kind in kinds:
                 send(kind, dest, 1, dest)
             return carry
@@ -163,7 +164,7 @@
                 pltpu.make_async_copy(src, dst, out_recv.at[kind, head]).start()
 
         def around(i):
-            return (chip + swing(i) + CHIPS) % CHIPS
+            return (chip + sign * swing(i) + CHIPS) % CHIPS
 
         @pl.when(turn == 0)
         def _():
@@ -268,6 +269,17 @@
     lax.fori_loop(0, HEADS, collect, 0)
 
 
+def hand_on(dq_ref, dk_ref, dv_ref, dq_out, dk_out, dv_out, sem):
+    copies = [
+        pltpu.make_async_copy(src, dst, sem.at[i])
+        for i, (src, dst) in enumerate(((dq_ref, dq_out), (dk_ref, dk_out), (dv_ref, dv_out)))
+    ]
+    for copy in copies:
+        copy.start()
+    for copy in copies:
+        copy.wait()
+
+
 def body(queries, keys, values, outputs, grad_out, log_norm, block_position):
     by_head = [jnp.transpose(x, (1, 0, 2)) for x in (queries, keys, values, outputs, grad_out)]
     whole = jax.ShapeDtypeStruct((HEADS, ROWS, WIDTH), jnp.bfloat16)
@@ -300,6 +312,15 @@
         ),
         name="attention_backward",
     )(*by_head, log_norm.T, block_position)
+    results = pl.pallas_call(
+        hand_on,
+        out_shape=(whole, whole, whole),
+        in_specs=[pl.BlockSpec(memory_space=pl.ANY)] * 3,
+        out_specs=[pl.BlockSpec(memory_space=pl.ANY)] * 3,
+        scratch_shapes=[pltpu.SemaphoreType.DMA((3,))],
+        compiler_params=pltpu.CompilerParams(vmem_limit_bytes=62 * 1024 * 1024),
+        name="hand_on",
+    )(*results)
     return tuple(jnp.transpose(x, (1, 0, 2)) for x in results)
 
 

time: 124 us -> 181 us (1.46)
  Pallas kernels: 119 us -> 180 us
  local copies, waits for them, and re-layouts: 4.21 us -> 0 us
    pallas_call x0 -> x1, Pallas kernels: none -> 60.7 us  [body(): pl.pallas_call(hand_on, out_shape=(whole, whole, whole), in_specs=[pl.Blo...]
    unnamed x7 -> x0, local copies, waits for them, and re-layouts: 4.21 us -> none
where the time goes in v3:
time: 181 us
  Pallas kernels  180 us (99%)
    pallas_call x1, Pallas kernels, body(): pl.pallas_call(kernel, out_shape=(whole, whole, whole), in_specs=[pl.Bloc...  120 us
    pallas_call x1, Pallas kernels, body(): pl.pallas_call(hand_on, out_shape=(whole, whole, whole), in_specs=[pl.Blo...  60.7 us

profile of v3, /device:TPU:1, one launch (start us, length us, event | category | flops | bytes accessed | tf_op | source)
XLA Modules:
  0.0 180.9 jit_solution(9845366756719946929)
XLA Ops:
  0.6 119.6 %attention_backward.1 = (bf16[20,128,128]{2,1,0:T(8,128)(2,1)}, bf16[20,128,128]{2,1,0:T(8,128)(2,1)}, bf16[20,128,128]{2,1,0:T(8,128)(2,1)}) custom-call(bf16[20,128,128]{2,1,0:T(8,128)(2,1)} %bitcast.9, bf16[20,128,128]{2,1,0:T(8,128)(2,1)} %bitcast.10, bf16[20,128,128]{2,1,0:T(8,128)(2,1)} %bitcast.11, bf16[20,128,128]{2,1,0:T(8,128)(2,1)} %bitcast.12, ...), custom_call_target="tpu_custom_call" | custom-call | tf_op jit(solution)/shard_map/attention_backward/pallas_call | solution.py:287
  120.3 60.7 %hand_on.1 = (bf16[20,128,128]{2,1,0:T(8,128)(2,1)}, bf16[20,128,128]{2,1,0:T(8,128)(2,1)}, bf16[20,128,128]{2,1,0:T(8,128)(2,1)}) custom-call(bf16[20,128,128]{2,1,0:T(8,128)(2,1)} %get-tuple-element.9.dq_ref, bf16[20,128,128]{2,1,0:T(8,128)(2,1)} %get-tuple-element.10.dk_ref, bf16[20,128,128]{2,1,0:T(8,128)(2,1)} %get-tuple-element.11.dv_ref), custom_call_target="tpu_custom_call" | custom-call | tf_op jit(solution)/shard_map/hand_on/pallas_call | solution.py:315

commit v4 on v2

--- a/solution.py
+++ b/solution.py
@@ -14,6 +14,7 @@
 EXTRA = HEADS - N
 STRIDE = N // EXTRA
 CHIPS = N // 2
+PIECES = 4
 PAIR = 2 * ROWS
 LOG2E = math.log2(math.e)
 SCALE = 1.0 / math.sqrt(WIDTH)
@@ -22,8 +23,14 @@
 DQ, DK, DV = range(3)
 
 
-def swing(step):
-    return (step + 1) // 2 * (2 * (step % 2) - 1)
+FAR_AND_NEAR = (4, 1, 5, 2, 7, 3, 6)
+
+
+def arrival(step):
+    offset = 0
+    for i, sent in enumerate(FAR_AND_NEAR):
+        offset = jnp.where(step == i + 1, CHIPS - sent, offset)
+    return offset
 
 
 def mm(a, b):
@@ -42,6 +49,7 @@
 ):
     me = lax.axis_index("ctx")
     chip = me // 2
+    core = me % 2
     two = me % STRIDE == 0
     extra_head = N + me // STRIDE
     sources = (k_ref, v_ref, q_ref, g_ref, auxs)
@@ -90,13 +98,13 @@
         for kind in kinds:
             keep(kind, me, 1)
 
-        def one(i, carry):
-            dest = (me + swing(i) + N) % N
+        dests = [2 * chip + 1 - core]
+        for offset in FAR_AND_NEAR:
+            for b in range(2):
+                dests.append(2 * ((chip + offset) % CHIPS) + (core + b) % 2)
+        for dest in dests:
             for kind in kinds:
                 send(kind, dest, 1, dest)
-            return carry
-
-        lax.fori_loop(1, N, one, 0)
 
     load_g = pltpu.make_async_copy(g_ref, gv, load_sem.at[0])
     load_o = pltpu.make_async_copy(o_ref, ov, load_sem.at[1])
@@ -163,7 +171,7 @@
                 pltpu.make_async_copy(src, dst, out_recv.at[kind, head]).start()
 
         def around(i):
-            return (chip + swing(i) + CHIPS) % CHIPS
+            return (chip + arrival(i)) % CHIPS
 
         @pl.when(turn == 0)
         def _():
@@ -268,6 +276,22 @@
     lax.fori_loop(0, HEADS, collect, 0)
 
 
+def hand_on(dq_ref, dk_ref, dv_ref, dq_out, dk_out, dv_out, held, load_sem, store_sem):
+    loads, stores = [], []
+    for i, (src, dst) in enumerate(((dq_ref, dq_out), (dk_ref, dk_out), (dv_ref, dv_out))):
+        for j in range(PIECES):
+            part = pl.ds(j * (HEADS // PIECES), HEADS // PIECES)
+            loads.append(pltpu.make_async_copy(src.at[part], held.at[i, part], load_sem.at[i, j]))
+            stores.append(pltpu.make_async_copy(held.at[i, part], dst.at[part], store_sem.at[i, j]))
+    for load in loads:
+        load.start()
+    for load, store in zip(loads, stores):
+        load.wait()
+        store.start()
+    for store in stores:
+        store.wait()
+
+
 def body(queries, keys, values, outputs, grad_out, log_norm, block_position):
     by_head = [jnp.transpose(x, (1, 0, 2)) for x in (queries, keys, values, outputs, grad_out)]
     whole = jax.ShapeDtypeStruct((HEADS, ROWS, WIDTH), jnp.bfloat16)
@@ -300,6 +324,19 @@
         ),
         name="attention_backward",
     )(*by_head, log_norm.T, block_position)
+    results = pl.pallas_call(
+        hand_on,
+        out_shape=(whole, whole, whole),
+        in_specs=[pl.BlockSpec(memory_space=pl.ANY)] * 3,
+        out_specs=[pl.BlockSpec(memory_space=pl.ANY)] * 3,
+        scratch_shapes=[
+            pltpu.VMEM((3, HEADS, ROWS, WIDTH), jnp.bfloat16),
+            pltpu.SemaphoreType.DMA((3, PIECES)),
+            pltpu.SemaphoreType.DMA((3, PIECES)),
+        ],
+        compiler_params=pltpu.CompilerParams(vmem_limit_bytes=62 * 1024 * 1024),
+        name="hand_on",
+    )(*results)
     return tuple(jnp.transpose(x, (1, 0, 2)) for x in results)
 
 

time: 124 us -> 123 us (level)
  local copies, waits for them, and re-layouts: 4.21 us -> 0 us
  Pallas kernels: 119 us -> 122 us
    unnamed x7 -> x0, local copies, waits for them, and re-layouts: 4.21 us -> none
    pallas_call x0 -> x1, Pallas kernels: none -> 2.49 us  [body(): pl.pallas_call(hand_on, out_shape=(whole, whole, whole), in_specs=[pl.Blo...]
where the time goes in v4:
time: 123 us; the launch traced here: 122 us
  Pallas kernels  122 us (99%)
    pallas_call x1, Pallas kernels, body(): pl.pallas_call(kernel, out_shape=(whole, whole, whole), in_specs=[pl.Bloc...  119 us
    pallas_call x1, Pallas kernels, body(): pl.pallas_call(hand_on, out_shape=(whole, whole, whole), in_specs=[pl.Blo...  2.49 us

profile of v4, /device:TPU:1, one launch (start us, length us, event | category | flops | bytes accessed | tf_op | source)
XLA Modules:
  0.0 122.3 jit_solution(15539474658185093122)
XLA Ops:
  0.6 119.2 %attention_backward.1 = (bf16[20,128,128]{2,1,0:T(8,128)(2,1)}, bf16[20,128,128]{2,1,0:T(8,128)(2,1)}, bf16[20,128,128]{2,1,0:T(8,128)(2,1)}) custom-call(bf16[20,128,128]{2,1,0:T(8,128)(2,1)} %bitcast.9, bf16[20,128,128]{2,1,0:T(8,128)(2,1)} %bitcast.10, bf16[20,128,128]{2,1,0:T(8,128)(2,1)} %bitcast.11, bf16[20,128,128]{2,1,0:T(8,128)(2,1)} %bitcast.12, ...), custom_call_target="tpu_custom_call" | custom-call | tf_op jit(solution)/shard_map/attention_backward/pallas_call | solution.py:299
  119.8 2.5 %hand_on.1 = (bf16[20,128,128]{2,1,0:T(8,128)(2,1)}, bf16[20,128,128]{2,1,0:T(8,128)(2,1)}, bf16[20,128,128]{2,1,0:T(8,128)(2,1)}) custom-call(bf16[20,128,128]{2,1,0:T(8,128)(2,1)} %get-tuple-element.9.dq_ref, bf16[20,128,128]{2,1,0:T(8,128)(2,1)} %get-tuple-element.10.dk_ref, bf16[20,128,128]{2,1,0:T(8,128)(2,1)} %get-tuple-element.11.dv_ref), custom_call_target="tpu_custom_call" | custom-call | tf_op jit(solution)/shard_map/hand_on/pallas_call | solution.py:327

commit v5 on v4

--- a/solution.py
+++ b/solution.py
@@ -12,8 +12,8 @@
 WIDTH = 128
 HEADS = 20
 EXTRA = HEADS - N
-STRIDE = N // EXTRA
 CHIPS = N // 2
+HALF = CHIPS // 2
 PIECES = 4
 PAIR = 2 * ROWS
 LOG2E = math.log2(math.e)
@@ -44,14 +44,15 @@
 def kernel(
     q_ref, k_ref, v_ref, o_ref, g_ref, ln_ref, pos_ref,
     dq_ref, dk_ref, dv_ref,
-    kb, vb, qb, gb, auxb, ov, gv, auxs, qt, gt, tri, dqa, dqo, dko, dvo,
-    load_sem, in_send, in_recv, out_send, out_recv,
+    kb, vb, qb, gb, auxb, ov, gv, auxs, qt, gt, tri, dqa, dqo, dko, dvo, dqn, part_out, part_in,
+    load_sem, in_send, in_recv, fwd_send, part_send, part_recv, out_send, out_recv,
 ):
     me = lax.axis_index("ctx")
     chip = me // 2
     core = me % 2
-    two = me % STRIDE == 0
-    extra_head = N + me // STRIDE
+    shares = core == 0
+    toward = 2 * (chip % 2) - 1
+    partner = me - 2 * toward
     sources = (k_ref, v_ref, q_ref, g_ref, auxs)
     landing = (kb, vb, qb, gb, auxb)
     staged = (dqo, dko, dvo)
@@ -59,6 +60,17 @@
 
     def wait(ref, sem):
         pltpu.make_async_copy(ref, ref, sem).wait()
+
+    def near(i):
+        return (chip + toward * i + CHIPS) % CHIPS
+
+    def far(i):
+        return (chip - toward * (i + 1) + CHIPS) % CHIPS
+
+    def nearer(which):
+        offset = (chip - 2 * which + CHIPS) % CHIPS
+        side = jnp.where((offset >= 1) & (offset <= CHIPS // 2), 1, 0)
+        return 2 * (2 * which + side)
 
     def send(kind, head, slot, dest):
         pltpu.make_async_remote_copy(
@@ -77,8 +89,8 @@
 
     def send_extra(kinds):
         def one(i, carry):
-            which = (me // STRIDE + i) % EXTRA
-            dest = which * STRIDE
+            which = (chip // 2 + i) % EXTRA
+            dest = nearer(which)
 
             @pl.when(dest != me)
             def _():
@@ -137,6 +149,26 @@
     send_extra((AUX,))
     send_main((AUX,))
     send_extra((K, V))
+
+    @pl.when(shares)
+    def _():
+        def forward(i, carry):
+            for b in range(2):
+                block = 2 * near(i) + b
+                for kind in (AUX, Q, G):
+                    wait(landing[kind].at[0, block], in_recv.at[kind, 0, block])
+                    pltpu.make_async_remote_copy(
+                        src_ref=landing[kind].at[0, block],
+                        dst_ref=landing[kind].at[0, block],
+                        send_sem=fwd_send.at[kind - Q, block],
+                        recv_sem=in_recv.at[kind, 0, block],
+                        device_id={"ctx": partner},
+                        device_id_type=pl.DeviceIdType.MESH,
+                    ).start()
+            return carry
+
+        lax.fori_loop(0, HALF, forward, 0)
+
     send_main((Q, G))
     send_main((K, V))
 
@@ -146,49 +178,75 @@
     tri[0] = jnp.zeros((ROWS, ROWS), jnp.float32)
     tri[1] = jnp.where(below, HIDE, 0.0)
 
+    def give(kind, slot, head, dest):
+        src = staged[kind].at[slot, dest]
+        dst = results[kind].at[head]
+
+        @pl.when(dest != me)
+        def _():
+            pltpu.make_async_remote_copy(
+                src_ref=src,
+                dst_ref=dst,
+                send_sem=out_send.at[kind, slot, dest],
+                recv_sem=out_recv.at[kind, head],
+                device_id={"ctx": dest},
+                device_id_type=pl.DeviceIdType.MESH,
+            ).start()
+
+        @pl.when(dest == me)
+        def _():
+            pltpu.make_async_copy(src, dst, out_recv.at[kind, head]).start()
+
+    def around(i):
+        return (chip + arrival(i)) % CHIPS
+
+    def pass_part(i):
+        return pltpu.make_async_remote_copy(
+            src_ref=part_out.at[i],
+            dst_ref=part_in.at[i],
+            send_sem=part_send.at[i],
+            recv_sem=part_recv.at[i],
+            device_id={"ctx": partner},
+            device_id_type=pl.DeviceIdType.MESH,
+        )
+
+    def turned(slot, c):
+        qt[c] = qb[slot, pl.ds(2 * c, 2)].reshape(PAIR, WIDTH).T
+        gt[c] = gb[slot, pl.ds(2 * c, 2)].reshape(PAIR, WIDTH).T
+
+    def queries_arrived(slot, c):
+        for b in range(2):
+            for kind in (AUX, Q, G):
+                wait(landing[kind].at[slot, 2 * c + b], in_recv.at[kind, slot, 2 * c + b])
+        turned(slot, c)
+
     def one_pair(step, carry):
-        slot = step // CHIPS
-        turn = step % CHIPS
-        head = jnp.where(slot == 0, extra_head, me)
-
-        def give(kind, dest):
-            src = staged[kind].at[slot, dest]
-            dst = results[kind].at[head]
-
-            @pl.when(dest != me)
-            def _():
-                pltpu.make_async_remote_copy(
-                    src_ref=src,
-                    dst_ref=dst,
-                    send_sem=out_send.at[kind, slot, dest],
-                    recv_sem=out_recv.at[kind, head],
-                    device_id={"ctx": dest},
-                    device_id_type=pl.DeviceIdType.MESH,
-                ).start()
-
-            @pl.when(dest == me)
-            def _():
-                pltpu.make_async_copy(src, dst, out_recv.at[kind, head]).start()
-
-        def around(i):
-            return (chip + arrival(i)) % CHIPS
+        slot = jnp.where(step < HALF, 0, 1)
+        turn = step - HALF * slot
+        head = jnp.where(slot == 0, N + chip // 2, me)
 
         @pl.when(turn == 0)
         def _():
             dqa[...] = jnp.zeros_like(dqa)
 
-            def arrived(i, carry):
-                c = around(i)
-                for b in range(2):
-                    for kind in (AUX, Q, G):
-                        wait(landing[kind].at[slot, 2 * c + b], in_recv.at[kind, slot, 2 * c + b])
-                qt[c] = qb[slot, pl.ds(2 * c, 2)].reshape(PAIR, WIDTH).T
-                gt[c] = gb[slot, pl.ds(2 * c, 2)].reshape(PAIR, WIDTH).T
+        @pl.when(step == 0)
+        def _():
+            def ready(i, carry):
+                turned(0, near(i))
+                queries_arrived(0, far(i))
                 return carry
 
-            lax.fori_loop(0, CHIPS, arrived, 0)
-
-        c = around(turn)
+            lax.fori_loop(0, HALF, ready, 0)
+
+        @pl.when(step == HALF)
+        def _():
+            def ready(i, carry):
+                queries_arrived(1, around(i))
+                return carry
+
+            lax.fori_loop(0, CHIPS, ready, 0)
+
+        c = jnp.where(slot == 0, near(turn), around(turn))
         for b in range(2):
             for kind in (K, V):
                 wait(landing[kind].at[slot, 2 * c + b], in_recv.at[kind, slot, 2 * c + b])
@@ -224,27 +282,50 @@
         dko[slot, pair] = (dk * SCALE).astype(jnp.bfloat16).reshape(2, ROWS, WIDTH)
         dvo[slot, pair] = dv.astype(jnp.bfloat16).reshape(2, ROWS, WIDTH)
         for b in range(2):
-            give(DK, 2 * c + b)
-            give(DV, 2 * c + b)
-
-        @pl.when(turn == CHIPS - 1)
+            give(DK, slot, head, 2 * c + b)
+            give(DV, slot, head, 2 * c + b)
+
+        @pl.when(step == HALF - 1)
+        def _():
+            def part(i, carry):
+                part_out[i] = dqa[far(i)].T.astype(jnp.bfloat16)
+                pass_part(i).start()
+                dqn[i] = dqa[near(i)].T
+                return carry
+
+            lax.fori_loop(0, HALF, part, 0)
+
+        @pl.when(shares & (step == HALF + 5))
+        def _():
+            def total(i, carry):
+                pass_part(i).wait_recv()
+                done = ((dqn[i] + part_in[i].astype(jnp.float32)) * SCALE).astype(jnp.bfloat16)
+                c = near(i)
+                dqo[0, pl.ds(2 * c, 2)] = done.reshape(2, ROWS, WIDTH)
+                for b in range(2):
+                    give(DQ, 0, N + chip // 2, 2 * c + b)
+                return carry
+
+            lax.fori_loop(0, HALF, total, 0)
+
+        @pl.when(step == HALF + CHIPS - 1)
         def _():
             def finish(i, carry):
                 c = around(i)
                 done = (dqa[c] * SCALE).T.astype(jnp.bfloat16)
-                dqo[slot, pl.ds(2 * c, 2)] = done.reshape(2, ROWS, WIDTH)
+                dqo[1, pl.ds(2 * c, 2)] = done.reshape(2, ROWS, WIDTH)
                 for b in range(2):
-                    give(DQ, 2 * c + b)
+                    give(DQ, 1, me, 2 * c + b)
                 return carry
 
             lax.fori_loop(0, CHIPS, finish, 0)
 
         return carry
 
-    lax.fori_loop(jnp.where(two, 0, CHIPS), 2 * CHIPS, one_pair, 0)
+    lax.fori_loop(jnp.where(shares, 0, HALF), HALF + CHIPS, one_pair, 0)
 
     def drain_in(h, carry):
-        owner = jnp.where(h < N, h, (h - N) * STRIDE)
+        owner = jnp.where(h < N, h, nearer(jnp.maximum(h - N, 0)))
 
         @pl.when(owner != me)
         def _():
@@ -255,18 +336,30 @@
 
     lax.fori_loop(0, HEADS, drain_in, 0)
 
-    def drain_out(step, carry):
-        slot = step // N
-        dest = step % N
-
+    def drain_out(slot, dest):
         @pl.when(dest != me)
         def _():
             for kind in range(3):
                 wait(staged[kind].at[slot, dest], out_send.at[kind, slot, dest])
 
+    def drain_main(dest, carry):
+        drain_out(1, dest)
         return carry
 
-    lax.fori_loop(jnp.where(two, 0, N), 2 * N, drain_out, 0)
+    lax.fori_loop(0, N, drain_main, 0)
+
+    @pl.when(shares)
+    def _():
+        def drain_shared(i, carry):
+            pass_part(i).wait_send()
+            for b in range(2):
+                block = 2 * near(i) + b
+                drain_out(0, block)
+                for kind in (AUX, Q, G):
+                    wait(landing[kind].at[0, block], fwd_send.at[kind - Q, block])
+            return carry
+
+        lax.fori_loop(0, HALF, drain_shared, 0)
 
     def collect(h, carry):
         for kind in range(3):
@@ -313,9 +406,15 @@
             pltpu.VMEM((2, ROWS, ROWS), jnp.float32),
             pltpu.VMEM((CHIPS, WIDTH, PAIR), jnp.float32),
             blocks, blocks, blocks,
+            pltpu.VMEM((HALF, PAIR, WIDTH), jnp.float32),
+            pltpu.VMEM((HALF, PAIR, WIDTH), jnp.bfloat16),
+            pltpu.VMEM((HALF, PAIR, WIDTH), jnp.bfloat16),
             pltpu.SemaphoreType.DMA((2,)),
             pltpu.SemaphoreType.DMA((5, HEADS)),
             pltpu.SemaphoreType.DMA((5, 2, N)),
+            pltpu.SemaphoreType.DMA((3, N)),
+            pltpu.SemaphoreType.DMA((HALF,)),
+            pltpu.SemaphoreType.DMA((HALF,)),
             pltpu.SemaphoreType.DMA((3, 2, N)),
             pltpu.SemaphoreType.DMA((3, HEADS)),
         ],

time: 123 us -> 118 us (0.959)
  Pallas kernels: 122 us -> 117 us
    pallas_call x1, Pallas kernels: 119 us -> 115 us  [body(): pl.pallas_call(kernel, out_shape=(whole, whole, whole), in_specs=[pl.Bloc...]
where the time goes in v5:
time: 118 us
  Pallas kernels  117 us (99%)
    pallas_call x1, Pallas kernels, body(): pl.pallas_call(kernel, out_shape=(whole, whole, whole), in_specs=[pl.Bloc...  115 us
    pallas_call x1, Pallas kernels, body(): pl.pallas_call(hand_on, out_shape=(whole, whole, whole), in_specs=[pl.Blo...  2.49 us

profile of v5, /device:TPU:1, one launch (start us, length us, event | category | flops | bytes accessed | tf_op | source)
XLA Modules:
  0.0 118.0 jit_solution(16512705790208623977)
XLA Ops:
  0.6 114.9 %attention_backward.1 = (bf16[20,128,128]{2,1,0:T(8,128)(2,1)}, bf16[20,128,128]{2,1,0:T(8,128)(2,1)}, bf16[20,128,128]{2,1,0:T(8,128)(2,1)}) custom-call(bf16[20,128,128]{2,1,0:T(8,128)(2,1)} %bitcast.9, bf16[20,128,128]{2,1,0:T(8,128)(2,1)} %bitcast.10, bf16[20,128,128]{2,1,0:T(8,128)(2,1)} %bitcast.11, bf16[20,128,128]{2,1,0:T(8,128)(2,1)} %bitcast.12, ...), custom_call_target="tpu_custom_call" | custom-call | tf_op jit(solution)/shard_map/attention_backward/pallas_call | solution.py:392
  115.6 2.5 %hand_on.1 = (bf16[20,128,128]{2,1,0:T(8,128)(2,1)}, bf16[20,128,128]{2,1,0:T(8,128)(2,1)}, bf16[20,128,128]{2,1,0:T(8,128)(2,1)}) custom-call(bf16[20,128,128]{2,1,0:T(8,128)(2,1)} %get-tuple-element.9.dq_ref, bf16[20,128,128]{2,1,0:T(8,128)(2,1)} %get-tuple-element.10.dk_ref, bf16[20,128,128]{2,1,0:T(8,128)(2,1)} %get-tuple-element.11.dv_ref), custom_call_target="tpu_custom_call" | custom-call | tf_op jit(solution)/shard_map/hand_on/pallas_call | solution.py:426

commit v6 on v5

--- a/solution.py
+++ b/solution.py
@@ -23,7 +23,7 @@
 DQ, DK, DV = range(3)
 
 
-FAR_AND_NEAR = (4, 1, 5, 2, 7, 3, 6)
+FAR_AND_NEAR = (1, 5, 2, 7, 3, 6, 4)
 
 
 def arrival(step):
@@ -44,8 +44,9 @@
 def kernel(
     q_ref, k_ref, v_ref, o_ref, g_ref, ln_ref, pos_ref,
     dq_ref, dk_ref, dv_ref,
-    kb, vb, qb, gb, auxb, ov, gv, auxs, qt, gt, tri, dqa, dqo, dko, dvo, dqn, part_out, part_in,
+    kb, vb, qb, gb, auxb, ov, gv, auxs, qt, gt, tri, dqa, dqo, dko, dvo, dqn, part_out, part_in, pass_in, pass_out,
     load_sem, in_send, in_recv, fwd_send, part_send, part_recv, out_send, out_recv,
+    pass_in_send, pass_in_recv, pass_out_send, pass_out_recv,
 ):
     me = lax.axis_index("ctx")
     chip = me // 2
@@ -53,6 +54,23 @@
     shares = core == 0
     toward = 2 * (chip % 2) - 1
     partner = me - 2 * toward
+    way = 2 - 4 * core
+    opposite = (chip + HALF) % CHIPS
+    by = 2 * ((chip + way + CHIPS) % CHIPS) + core
+    passed_from = 2 * ((chip - way + CHIPS) % CHIPS) + core
+
+    def passed_to(b):
+        return 2 * ((chip + way + CHIPS) % CHIPS) + (core + b) % 2
+
+    def remote(src, dst, send_sem, recv_sem, dest):
+        return pltpu.make_async_remote_copy(
+            src_ref=src,
+            dst_ref=dst,
+            send_sem=send_sem,
+            recv_sem=recv_sem,
+            device_id={"ctx": dest},
+            device_id_type=pl.DeviceIdType.MESH,
+        )
     sources = (k_ref, v_ref, q_ref, g_ref, auxs)
     landing = (kb, vb, qb, gb, auxb)
     staged = (dqo, dko, dvo)
@@ -110,13 +128,40 @@
         for kind in kinds:
             keep(kind, me, 1)
 
+        if AUX not in kinds:
+            for b in range(2):
+                dest = 2 * opposite + (core + b) % 2
+                for kind in kinds:
+                    remote(
+                        sources[kind].at[dest], pass_in.at[kind, b],
+                        in_send.at[kind, dest], pass_in_recv.at[kind, b], by,
+                    ).start()
         dests = [2 * chip + 1 - core]
         for offset in FAR_AND_NEAR:
-            for b in range(2):
-                dests.append(2 * ((chip + offset) % CHIPS) + (core + b) % 2)
+            if offset != HALF or AUX in kinds:
+                for b in range(2):
+                    dests.append(2 * ((chip + offset) % CHIPS) + (core + b) % 2)
         for dest in dests:
             for kind in kinds:
                 send(kind, dest, 1, dest)
+
+    def pass_inputs(kinds):
+        for b in range(2):
+            for kind in kinds:
+                wait(pass_in.at[kind, b], pass_in_recv.at[kind, b])
+                remote(
+                    pass_in.at[kind, b], landing[kind].at[1, passed_from],
+                    pass_in_send.at[kind, b], in_recv.at[kind, 1, passed_from], passed_to(b),
+                ).start()
+
+    def pass_results(kinds):
+        for kind in kinds:
+            for b in range(2):
+                wait(pass_out.at[kind, b], pass_out_recv.at[kind, b])
+                remote(
+                    pass_out.at[kind, b], results[kind].at[passed_from],
+                    pass_out_send.at[kind, b], out_recv.at[kind, passed_from], passed_to(b),
+                ).start()
 
     load_g = pltpu.make_async_copy(g_ref, gv, load_sem.at[0])
     load_o = pltpu.make_async_copy(o_ref, ov, load_sem.at[1])
@@ -170,6 +215,7 @@
         lax.fori_loop(0, HALF, forward, 0)
 
     send_main((Q, G))
+    pass_inputs((Q, G))
     send_main((K, V))
 
     below = lax.broadcasted_iota(jnp.int32, (ROWS, ROWS), 0) > lax.broadcasted_iota(
@@ -182,15 +228,19 @@
         src = staged[kind].at[slot, dest]
         dst = results[kind].at[head]
 
-        @pl.when(dest != me)
-        def _():
-            pltpu.make_async_remote_copy(
-                src_ref=src,
-                dst_ref=dst,
-                send_sem=out_send.at[kind, slot, dest],
-                recv_sem=out_recv.at[kind, head],
-                device_id={"ctx": dest},
-                device_id_type=pl.DeviceIdType.MESH,
+        passed = (slot == 1) & (dest // 2 == opposite)
+
+        @pl.when(passed)
+        def _():
+            b = (dest + core) % 2
+            remote(
+                src, pass_out.at[kind, b], out_send.at[kind, slot, dest], pass_out_recv.at[kind, b], by
+            ).start()
+
+        @pl.when((dest != me) & jnp.logical_not(passed))
+        def _():
+            remote(
+                src, dst, out_send.at[kind, slot, dest], out_recv.at[kind, head], dest
             ).start()
 
         @pl.when(dest == me)
@@ -245,6 +295,7 @@
                 return carry
 
             lax.fori_loop(0, CHIPS, ready, 0)
+            pass_inputs((K, V))
 
         c = jnp.where(slot == 0, near(turn), around(turn))
         for b in range(2):
@@ -311,7 +362,7 @@
         @pl.when(step == HALF + CHIPS - 1)
         def _():
             def finish(i, carry):
-                c = around(i)
+                c = around((i + CHIPS - 1) % CHIPS)
                 done = (dqa[c] * SCALE).T.astype(jnp.bfloat16)
                 dqo[1, pl.ds(2 * c, 2)] = done.reshape(2, ROWS, WIDTH)
                 for b in range(2):
@@ -323,6 +374,7 @@
         return carry
 
     lax.fori_loop(jnp.where(shares, 0, HALF), HALF + CHIPS, one_pair, 0)
+    pass_results((DK, DV, DQ))
 
     def drain_in(h, carry):
         owner = jnp.where(h < N, h, nearer(jnp.maximum(h - N, 0)))
@@ -367,6 +419,11 @@
         return carry
 
     lax.fori_loop(0, HEADS, collect, 0)
+    for b in range(2):
+        for kind in (K, V, Q, G):
+            wait(pass_in.at[kind, b], pass_in_send.at[kind, b])
+        for kind in (DQ, DK, DV):
+            wait(pass_out.at[kind, b], pass_out_send.at[kind, b])
 
 
 def hand_on(dq_ref, dk_ref, dv_ref, dq_out, dk_out, dv_out, held, load_sem, store_sem):
@@ -409,6 +466,8 @@
             pltpu.VMEM((HALF, PAIR, WIDTH), jnp.float32),
             pltpu.VMEM((HALF, PAIR, WIDTH), jnp.bfloat16),
             pltpu.VMEM((HALF, PAIR, WIDTH), jnp.bfloat16),
+            pltpu.VMEM((4, 2, ROWS, WIDTH), jnp.bfloat16),
+            pltpu.VMEM((3, 2, ROWS, WIDTH), jnp.bfloat16),
             pltpu.SemaphoreType.DMA((2,)),
             pltpu.SemaphoreType.DMA((5, HEADS)),
             pltpu.SemaphoreType.DMA((5, 2, N)),
@@ -417,6 +476,10 @@
             pltpu.SemaphoreType.DMA((HALF,)),
             pltpu.SemaphoreType.DMA((3, 2, N)),
             pltpu.SemaphoreType.DMA((3, HEADS)),
+            pltpu.SemaphoreType.DMA((4, 2)),
+            pltpu.SemaphoreType.DMA((4, 2)),
+            pltpu.SemaphoreType.DMA((3, 2)),
+            pltpu.SemaphoreType.DMA((3, 2)),
         ],
         compiler_params=pltpu.CompilerParams(
             collective_id=0, has_side_effects=True, vmem_limit_bytes=62 * 1024 * 1024

time: 118 us -> 119 us (level)
  Pallas kernels: 117 us -> 119 us
    pallas_call x1, Pallas kernels: 115 us -> 116 us  [body(): pl.pallas_call(kernel, out_shape=(whole, whole, whole), in_specs=[pl.Bloc...]
where the time goes in v6:
time: 119 us
  Pallas kernels  119 us (100%)
    pallas_call x1, Pallas kernels, body(): pl.pallas_call(kernel, out_shape=(whole, whole, whole), in_specs=[pl.Bloc...  116 us
    pallas_call x1, Pallas kernels, body(): pl.pallas_call(hand_on, out_shape=(whole, whole, whole), in_specs=[pl.Blo...  2.49 us

profile of v6, /device:TPU:1, one launch (start us, length us, event | category | flops | bytes accessed | tf_op | source)
XLA Modules:
  0.0 119.3 jit_solution(1612338838509966107)
XLA Ops:
  0.6 116.2 %attention_backward.1 = (bf16[20,128,128]{2,1,0:T(8,128)(2,1)}, bf16[20,128,128]{2,1,0:T(8,128)(2,1)}, bf16[20,128,128]{2,1,0:T(8,128)(2,1)}) custom-call(bf16[20,128,128]{2,1,0:T(8,128)(2,1)} %bitcast.9, bf16[20,128,128]{2,1,0:T(8,128)(2,1)} %bitcast.10, bf16[20,128,128]{2,1,0:T(8,128)(2,1)} %bitcast.11, bf16[20,128,128]{2,1,0:T(8,128)(2,1)} %bitcast.12, ...), custom_call_target="tpu_custom_call" | custom-call | tf_op jit(solution)/shard_map/attention_backward/pallas_call | solution.py:449
  116.8 2.5 %hand_on.1 = (bf16[20,128,128]{2,1,0:T(8,128)(2,1)}, bf16[20,128,128]{2,1,0:T(8,128)(2,1)}, bf16[20,128,128]{2,1,0:T(8,128)(2,1)}) custom-call(bf16[20,128,128]{2,1,0:T(8,128)(2,1)} %get-tuple-element.9.dq_ref, bf16[20,128,128]{2,1,0:T(8,128)(2,1)} %get-tuple-element.10.dk_ref, bf16[20,128,128]{2,1,0:T(8,128)(2,1)} %get-tuple-element.11.dv_ref), custom_call_target="tpu_custom_call" | custom-call | tf_op jit(solution)/shard_map/hand_on/pallas_call | solution.py:489

commit v7 on v5

--- a/solution.py
+++ b/solution.py
@@ -14,7 +14,6 @@
 EXTRA = HEADS - N
 CHIPS = N // 2
 HALF = CHIPS // 2
-PIECES = 4
 PAIR = 2 * ROWS
 LOG2E = math.log2(math.e)
 SCALE = 1.0 / math.sqrt(WIDTH)
@@ -87,34 +86,29 @@
             sources[kind].at[head], landing[kind].at[slot, me], in_recv.at[kind, slot, me]
         ).start()
 
-    def send_extra(kinds):
-        def one(i, carry):
-            which = (chip // 2 + i) % EXTRA
-            dest = nearer(which)
-
-            @pl.when(dest != me)
-            def _():
-                for kind in kinds:
-                    send(kind, N + which, 0, dest)
-
-            @pl.when(dest == me)
-            def _():
-                for kind in kinds:
-                    keep(kind, N + which, 0)
-
-            return carry
-
-        lax.fori_loop(0, EXTRA, one, 0)
-
-    def send_main(kinds):
+    def send_extra(kinds, i):
+        which = (chip // 2 + i) % EXTRA
+        dest = nearer(which)
+
+        @pl.when(dest != me)
+        def _():
+            for kind in kinds:
+                send(kind, N + which, 0, dest)
+
+        @pl.when(dest == me)
+        def _():
+            for kind in kinds:
+                keep(kind, N + which, 0)
+
+    def send_own_chip(kinds):
         for kind in kinds:
             keep(kind, me, 1)
-
-        dests = [2 * chip + 1 - core]
-        for offset in FAR_AND_NEAR:
-            for b in range(2):
-                dests.append(2 * ((chip + offset) % CHIPS) + (core + b) % 2)
-        for dest in dests:
+        for kind in kinds:
+            send(kind, 2 * chip + 1 - core, 1, 2 * chip + 1 - core)
+
+    def send_main(kinds, i):
+        for b in range(2):
+            dest = 2 * ((chip + FAR_AND_NEAR[i]) % CHIPS) + (core + b) % 2
             for kind in kinds:
                 send(kind, dest, 1, dest)
 
@@ -133,7 +127,10 @@
     lax.fori_loop(1, N, greet, 0)
     pl.semaphore_wait(barrier, N - 1)
 
-    send_extra((Q, G))
+    send_own_chip((Q, G))
+    for i in range(2):
+        send_main((Q, G), i)
+        send_extra((Q, G), i)
 
     load_g.wait()
     load_o.wait()
@@ -146,9 +143,17 @@
         low = (product - high.astype(jnp.float32)).astype(jnp.bfloat16)
         delta = (mm_nt(ones, high) + mm_nt(ones, low)).astype(jnp.bfloat16).astype(jnp.float32)
         auxs[h] = jnp.where(upper, norm[h : h + 1, :], delta)
-    send_extra((AUX,))
-    send_main((AUX,))
-    send_extra((K, V))
+    for i in range(EXTRA):
+        send_extra((AUX,), i)
+    send_own_chip((AUX,))
+    for i in range(CHIPS - 1):
+        send_main((AUX,), i)
+    for i in range(2, CHIPS - 1):
+        send_main((Q, G), i)
+        if i < EXTRA:
+            send_extra((Q, G), i)
+        if i < 2 + EXTRA:
+            send_extra((K, V), i - 2)
 
     @pl.when(shares)
     def _():
@@ -169,8 +174,9 @@
 
         lax.fori_loop(0, HALF, forward, 0)
 
-    send_main((Q, G))
-    send_main((K, V))
+    send_own_chip((K, V))
+    for i in range(CHIPS - 1):
+        send_main((K, V), i)
 
     below = lax.broadcasted_iota(jnp.int32, (ROWS, ROWS), 0) > lax.broadcasted_iota(
         jnp.int32, (ROWS, ROWS), 1
@@ -369,32 +375,28 @@
     lax.fori_loop(0, HEADS, collect, 0)
 
 
-def hand_on(dq_ref, dk_ref, dv_ref, dq_out, dk_out, dv_out, held, load_sem, store_sem):
-    loads, stores = [], []
-    for i, (src, dst) in enumerate(((dq_ref, dq_out), (dk_ref, dk_out), (dv_ref, dv_out))):
-        for j in range(PIECES):
-            part = pl.ds(j * (HEADS // PIECES), HEADS // PIECES)
-            loads.append(pltpu.make_async_copy(src.at[part], held.at[i, part], load_sem.at[i, j]))
-            stores.append(pltpu.make_async_copy(held.at[i, part], dst.at[part], store_sem.at[i, j]))
-    for load in loads:
-        load.start()
-    for load, store in zip(loads, stores):
-        load.wait()
-        store.start()
-    for store in stores:
-        store.wait()
+def hand_on(dq_ref, dk_ref, dv_ref, dq_out, dk_out, dv_out, sem):
+    copies = [
+        pltpu.make_async_copy(src, dst, sem.at[i])
+        for i, (src, dst) in enumerate(((dq_ref, dq_out), (dk_ref, dk_out), (dv_ref, dv_out)))
+    ]
+    for copy in copies:
+        copy.start()
+    for copy in copies:
+        copy.wait()
 
 
 def body(queries, keys, values, outputs, grad_out, log_norm, block_position):
     by_head = [jnp.transpose(x, (1, 0, 2)) for x in (queries, keys, values, outputs, grad_out)]
     whole = jax.ShapeDtypeStruct((HEADS, ROWS, WIDTH), jnp.bfloat16)
+    landed = pltpu.VMEM((HEADS, ROWS, WIDTH), jnp.bfloat16)
     blocks = pltpu.VMEM((2, N, ROWS, WIDTH), jnp.bfloat16)
     results = pl.pallas_call(
         kernel,
-        out_shape=(whole, whole, whole),
+        out_shape=(landed, landed, landed),
         in_specs=[pl.BlockSpec(memory_space=pl.ANY)] * 5
         + [pl.BlockSpec(memory_space=pltpu.VMEM), pl.BlockSpec(memory_space=pltpu.SMEM)],
-        out_specs=[pl.BlockSpec(memory_space=pl.ANY)] * 3,
+        out_specs=[pl.BlockSpec(memory_space=pltpu.VMEM)] * 3,
         scratch_shapes=[
             blocks, blocks, blocks, blocks,
             pltpu.VMEM((2, N, 8, ROWS), jnp.float32),
@@ -419,21 +421,17 @@
             pltpu.SemaphoreType.DMA((3, HEADS)),
         ],
         compiler_params=pltpu.CompilerParams(
-            collective_id=0, has_side_effects=True, vmem_limit_bytes=62 * 1024 * 1024
+            collective_id=0, has_side_effects=True, vmem_limit_bytes=60 * 1024 * 1024
         ),
         name="attention_backward",
     )(*by_head, log_norm.T, block_position)
     results = pl.pallas_call(
         hand_on,
         out_shape=(whole, whole, whole),
-        in_specs=[pl.BlockSpec(memory_space=pl.ANY)] * 3,
+        in_specs=[pl.BlockSpec(memory_space=pltpu.VMEM)] * 3,
         out_specs=[pl.BlockSpec(memory_space=pl.ANY)] * 3,
-        scratch_shapes=[
-            pltpu.VMEM((3, HEADS, ROWS, WIDTH), jnp.bfloat16),
-            pltpu.SemaphoreType.DMA((3, PIECES)),
-            pltpu.SemaphoreType.DMA((3, PIECES)),
-        ],
-        compiler_params=pltpu.CompilerParams(vmem_limit_bytes=62 * 1024 * 1024),
+        scratch_shapes=[pltpu.SemaphoreType.DMA((3,))],
+        compiler_params=pltpu.CompilerParams(vmem_limit_bytes=8 * 1024 * 1024),
         name="hand_on",
     )(*results)
     return tuple(jnp.transpose(x, (1, 0, 2)) for x in results)

time: 118 us -> 118 us (level)
    pallas_call x1, Pallas kernels: 2.49 us -> 1.3 us  [body(): pl.pallas_call(hand_on, out_shape=(whole, whole, whole), in_specs=[pl.Blo...]
where the time goes in v7:
time: 118 us; the launch traced here: 117 us
  Pallas kernels  117 us (99%)
    pallas_call x1, Pallas kernels, body(): pl.pallas_call(kernel, out_shape=(landed, landed, landed), in_specs=[pl.B...  115 us

profile of v7, /device:TPU:1, one launch (start us, length us, event | category | flops | bytes accessed | tf_op | source)
XLA Modules:
  0.0 117.4 jit_solution(6581269441117876132)
XLA Ops:
  0.6 115.5 %attention_backward.1 = (bf16[20,128,128]{2,1,0:T(8,128)(2,1)S(1)}, bf16[20,128,128]{2,1,0:T(8,128)(2,1)S(1)}, bf16[20,128,128]{2,1,0:T(8,128)(2,1)S(1)}) custom-call(bf16[20,128,128]{2,1,0:T(8,128)(2,1)} %bitcast.9, bf16[20,128,128]{2,1,0:T(8,128)(2,1)} %bitcast.10, bf16[20,128,128]{2,1,0:T(8,128)(2,1)} %bitcast.11, bf16[20,128,128]{2,1,0:T(8,128)(2,1)} %bitcast.12, ...), custom_call_target="tpu_custom_call" | custom-call | tf_op jit(solution)/shard_map/attention_backward/pallas_call | solution.py:394
  116.1 1.3 %hand_on.1 = (bf16[20,128,128]{2,1,0:T(8,128)(2,1)}, bf16[20,128,128]{2,1,0:T(8,128)(2,1)}, bf16[20,128,128]{2,1,0:T(8,128)(2,1)}) custom-call(bf16[20,128,128]{2,1,0:T(8,128)(2,1)S(1)} %get-tuple-element.9.dq_ref, bf16[20,128,128]{2,1,0:T(8,128)(2,1)S(1)} %get-tuple-element.10.dk_ref, bf16[20,128,128]{2,1,0:T(8,128)(2,1)S(1)} %get-tuple-element.11.dv_ref), custom_call_target="tpu_custom_call" | custom-call | tf_op jit(solution)/shard_map/hand_on/pallas_call | solution.py:428

commit v8 on v7

--- a/solution.py
+++ b/solution.py
@@ -18,8 +18,8 @@
 LOG2E = math.log2(math.e)
 SCALE = 1.0 / math.sqrt(WIDTH)
 HIDE = 1e30
-K, V, Q, G, AUX = range(5)
-DQ, DK, DV = range(3)
+KV, QG, AUX = range(3)
+DQ, DKV = range(2)
 
 
 FAR_AND_NEAR = (4, 1, 5, 2, 7, 3, 6)
@@ -42,8 +42,8 @@
 
 def kernel(
     q_ref, k_ref, v_ref, o_ref, g_ref, ln_ref, pos_ref,
-    dq_ref, dk_ref, dv_ref,
-    kb, vb, qb, gb, auxb, ov, gv, auxs, qt, gt, tri, dqa, dqo, dko, dvo, dqn, part_out, part_in,
+    dq_ref, dkv_ref,
+    kv, qg, auxs, kvb, qgb, auxb, ov, qt, gt, tri, dqa, dqo, dkvo, dqn, part_out, part_in,
     load_sem, in_send, in_recv, fwd_send, part_send, part_recv, out_send, out_recv,
 ):
     me = lax.axis_index("ctx")
@@ -52,10 +52,10 @@
     shares = core == 0
     toward = 2 * (chip % 2) - 1
     partner = me - 2 * toward
-    sources = (k_ref, v_ref, q_ref, g_ref, auxs)
-    landing = (kb, vb, qb, gb, auxb)
-    staged = (dqo, dko, dvo)
-    results = (dq_ref, dk_ref, dv_ref)
+    sources = (kv, qg, auxs)
+    landing = (kvb, qgb, auxb)
+    staged = (dqo, dkvo)
+    results = (dq_ref, dkv_ref)
 
     def wait(ref, sem):
         pltpu.make_async_copy(ref, ref, sem).wait()
@@ -112,10 +112,20 @@
             for kind in kinds:
                 send(kind, dest, 1, dest)
 
-    load_g = pltpu.make_async_copy(g_ref, gv, load_sem.at[0])
-    load_o = pltpu.make_async_copy(o_ref, ov, load_sem.at[1])
-    load_g.start()
-    load_o.start()
+    loads = [
+        pltpu.make_async_copy(src, dst, load_sem.at[i])
+        for i, (src, dst) in enumerate(
+            (
+                (q_ref, qg.at[:, 0]),
+                (g_ref, qg.at[:, 1]),
+                (o_ref, ov),
+                (k_ref, kv.at[:, 0]),
+                (v_ref, kv.at[:, 1]),
+            )
+        )
+    ]
+    for load in loads:
+        load.start()
     barrier = pltpu.get_barrier_semaphore()
 
     def greet(i, carry):
@@ -127,18 +137,19 @@
     lax.fori_loop(1, N, greet, 0)
     pl.semaphore_wait(barrier, N - 1)
 
-    send_own_chip((Q, G))
+    loads[0].wait()
+    loads[1].wait()
+    send_own_chip((QG,))
     for i in range(2):
-        send_main((Q, G), i)
-        send_extra((Q, G), i)
-
-    load_g.wait()
-    load_o.wait()
+        send_main((QG,), i)
+        send_extra((QG,), i)
+
+    loads[2].wait()
     norm = ln_ref[...].astype(jnp.float32) * LOG2E
     ones = jnp.ones((8, WIDTH), jnp.bfloat16)
     upper = lax.broadcasted_iota(jnp.int32, (8, ROWS), 0) < 4
     for h in range(HEADS):
-        product = gv[h].astype(jnp.float32) * ov[h].astype(jnp.float32)
+        product = qg[h, 1].astype(jnp.float32) * ov[h].astype(jnp.float32)
         high = product.astype(jnp.bfloat16)
         low = (product - high.astype(jnp.float32)).astype(jnp.bfloat16)
         delta = (mm_nt(ones, high) + mm_nt(ones, low)).astype(jnp.bfloat16).astype(jnp.float32)
@@ -148,24 +159,26 @@
     send_own_chip((AUX,))
     for i in range(CHIPS - 1):
         send_main((AUX,), i)
+    loads[3].wait()
+    loads[4].wait()
     for i in range(2, CHIPS - 1):
-        send_main((Q, G), i)
+        send_main((QG,), i)
         if i < EXTRA:
-            send_extra((Q, G), i)
+            send_extra((QG,), i)
         if i < 2 + EXTRA:
-            send_extra((K, V), i - 2)
+            send_extra((KV,), i - 2)
 
     @pl.when(shares)
     def _():
         def forward(i, carry):
             for b in range(2):
                 block = 2 * near(i) + b
-                for kind in (AUX, Q, G):
+                for kind in (AUX, QG):
                     wait(landing[kind].at[0, block], in_recv.at[kind, 0, block])
                     pltpu.make_async_remote_copy(
                         src_ref=landing[kind].at[0, block],
                         dst_ref=landing[kind].at[0, block],
-                        send_sem=fwd_send.at[kind - Q, block],
+                        send_sem=fwd_send.at[kind - QG, block],
                         recv_sem=in_recv.at[kind, 0, block],
                         device_id={"ctx": partner},
                         device_id_type=pl.DeviceIdType.MESH,
@@ -174,9 +187,9 @@
 
         lax.fori_loop(0, HALF, forward, 0)
 
-    send_own_chip((K, V))
+    send_own_chip((KV,))
     for i in range(CHIPS - 1):
-        send_main((K, V), i)
+        send_main((KV,), i)
 
     below = lax.broadcasted_iota(jnp.int32, (ROWS, ROWS), 0) > lax.broadcasted_iota(
         jnp.int32, (ROWS, ROWS), 1
@@ -217,12 +230,12 @@
         )
 
     def turned(slot, c):
-        qt[c] = qb[slot, pl.ds(2 * c, 2)].reshape(PAIR, WIDTH).T
-        gt[c] = gb[slot, pl.ds(2 * c, 2)].reshape(PAIR, WIDTH).T
+        qt[c] = qgb[slot, pl.ds(2 * c, 2), 0].reshape(PAIR, WIDTH).T
+        gt[c] = qgb[slot, pl.ds(2 * c, 2), 1].reshape(PAIR, WIDTH).T
 
     def queries_arrived(slot, c):
         for b in range(2):
-            for kind in (AUX, Q, G):
+            for kind in (AUX, QG):
                 wait(landing[kind].at[slot, 2 * c + b], in_recv.at[kind, slot, 2 * c + b])
         turned(slot, c)
 
@@ -254,18 +267,18 @@
 
         c = jnp.where(slot == 0, near(turn), around(turn))
         for b in range(2):
-            for kind in (K, V):
+            for kind in (KV,):
                 wait(landing[kind].at[slot, 2 * c + b], in_recv.at[kind, slot, 2 * c + b])
         pair = pl.ds(2 * c, 2)
-        keys = kb[slot, pair].reshape(PAIR, WIDTH)
-        vals = vb[slot, pair].reshape(PAIR, WIDTH)
+        keys = kvb[slot, pair, 0].reshape(PAIR, WIDTH)
+        vals = kvb[slot, pair, 1].reshape(PAIR, WIDTH)
         keys_t = keys.T
         dk = jnp.zeros((PAIR, WIDTH), jnp.float32)
         dv = jnp.zeros((PAIR, WIDTH), jnp.float32)
         for t in range(CHIPS):
             spot = slice(2 * t, 2 * t + 2)
-            queries = qb[slot, spot].reshape(PAIR, WIDTH)
-            grads = gb[slot, spot].reshape(PAIR, WIDTH)
+            queries = qgb[slot, spot, 0].reshape(PAIR, WIDTH)
+            grads = qgb[slot, spot, 1].reshape(PAIR, WIDTH)
             norms = [auxb[slot, 2 * t + b, 0:1, :] for b in range(2)]
             delta = jnp.concatenate([auxb[slot, 2 * t + b, 4:5, :] for b in range(2)], axis=1)
             diagonal = tri[jnp.where(c == t, 1, 0)]
@@ -285,11 +298,10 @@
             dv += mm(weights.astype(jnp.bfloat16), grads)
             dk += mm(grad_scores, queries)
             dqa[t] += mm(keys_t, grad_scores)
-        dko[slot, pair] = (dk * SCALE).astype(jnp.bfloat16).reshape(2, ROWS, WIDTH)
-        dvo[slot, pair] = dv.astype(jnp.bfloat16).reshape(2, ROWS, WIDTH)
+        dkvo[slot, pair, 0] = (dk * SCALE).astype(jnp.bfloat16).reshape(2, ROWS, WIDTH)
+        dkvo[slot, pair, 1] = dv.astype(jnp.bfloat16).reshape(2, ROWS, WIDTH)
         for b in range(2):
-            give(DK, slot, head, 2 * c + b)
-            give(DV, slot, head, 2 * c + b)
+            give(DKV, slot, head, 2 * c + b)
 
         @pl.when(step == HALF - 1)
         def _():
@@ -335,7 +347,7 @@
 
         @pl.when(owner != me)
         def _():
-            for kind in range(5):
+            for kind in range(3):
                 wait(sources[kind].at[h], in_send.at[kind, h])
 
         return carry
@@ -345,7 +357,7 @@
     def drain_out(slot, dest):
         @pl.when(dest != me)
         def _():
-            for kind in range(3):
+            for kind in range(2):
                 wait(staged[kind].at[slot, dest], out_send.at[kind, slot, dest])
 
     def drain_main(dest, carry):
@@ -361,24 +373,26 @@
             for b in range(2):
                 block = 2 * near(i) + b
                 drain_out(0, block)
-                for kind in (AUX, Q, G):
-                    wait(landing[kind].at[0, block], fwd_send.at[kind - Q, block])
+                for kind in (AUX, QG):
+                    wait(landing[kind].at[0, block], fwd_send.at[kind - QG, block])
             return carry
 
         lax.fori_loop(0, HALF, drain_shared, 0)
 
     def collect(h, carry):
-        for kind in range(3):
+        for kind in range(2):
             wait(results[kind].at[h], out_recv.at[kind, h])
         return carry
 
     lax.fori_loop(0, HEADS, collect, 0)
 
 
-def hand_on(dq_ref, dk_ref, dv_ref, dq_out, dk_out, dv_out, sem):
+def hand_on(dq_ref, dkv_ref, dq_out, dk_out, dv_out, sem):
     copies = [
         pltpu.make_async_copy(src, dst, sem.at[i])
-        for i, (src, dst) in enumerate(((dq_ref, dq_out), (dk_ref, dk_out), (dv_ref, dv_out)))
+        for i, (src, dst) in enumerate(
+            ((dq_ref, dq_out), (dkv_ref.at[:, 0], dk_out), (dkv_ref.at[:, 1], dv_out))
+        )
     ]
     for copy in copies:
         copy.start()
@@ -389,36 +403,37 @@
 def body(queries, keys, values, outputs, grad_out, log_norm, block_position):
     by_head = [jnp.transpose(x, (1, 0, 2)) for x in (queries, keys, values, outputs, grad_out)]
     whole = jax.ShapeDtypeStruct((HEADS, ROWS, WIDTH), jnp.bfloat16)
-    landed = pltpu.VMEM((HEADS, ROWS, WIDTH), jnp.bfloat16)
+    doubles = pltpu.VMEM((HEADS, 2, ROWS, WIDTH), jnp.bfloat16)
     blocks = pltpu.VMEM((2, N, ROWS, WIDTH), jnp.bfloat16)
+    double_blocks = pltpu.VMEM((2, N, 2, ROWS, WIDTH), jnp.bfloat16)
     results = pl.pallas_call(
         kernel,
-        out_shape=(landed, landed, landed),
+        out_shape=(pltpu.VMEM((HEADS, ROWS, WIDTH), jnp.bfloat16), doubles),
         in_specs=[pl.BlockSpec(memory_space=pl.ANY)] * 5
         + [pl.BlockSpec(memory_space=pltpu.VMEM), pl.BlockSpec(memory_space=pltpu.SMEM)],
-        out_specs=[pl.BlockSpec(memory_space=pltpu.VMEM)] * 3,
+        out_specs=[pl.BlockSpec(memory_space=pltpu.VMEM)] * 2,
         scratch_shapes=[
-            blocks, blocks, blocks, blocks,
+            doubles, doubles,
+            pltpu.VMEM((HEADS, 8, ROWS), jnp.float32),
+            double_blocks, double_blocks,
             pltpu.VMEM((2, N, 8, ROWS), jnp.float32),
             pltpu.VMEM((HEADS, ROWS, WIDTH), jnp.bfloat16),
-            pltpu.VMEM((HEADS, ROWS, WIDTH), jnp.bfloat16),
-            pltpu.VMEM((HEADS, 8, ROWS), jnp.float32),
             pltpu.VMEM((CHIPS, WIDTH, PAIR), jnp.bfloat16),
             pltpu.VMEM((CHIPS, WIDTH, PAIR), jnp.bfloat16),
             pltpu.VMEM((2, ROWS, ROWS), jnp.float32),
             pltpu.VMEM((CHIPS, WIDTH, PAIR), jnp.float32),
-            blocks, blocks, blocks,
+            blocks, double_blocks,
             pltpu.VMEM((HALF, PAIR, WIDTH), jnp.float32),
             pltpu.VMEM((HALF, PAIR, WIDTH), jnp.bfloat16),
             pltpu.VMEM((HALF, PAIR, WIDTH), jnp.bfloat16),
-            pltpu.SemaphoreType.DMA((2,)),
-            pltpu.SemaphoreType.DMA((5, HEADS)),
-            pltpu.SemaphoreType.DMA((5, 2, N)),
-            pltpu.SemaphoreType.DMA((3, N)),
+            pltpu.SemaphoreType.DMA((5,)),
+            pltpu.SemaphoreType.DMA((3, HEADS)),
+            pltpu.SemaphoreType.DMA((3, 2, N)),
+            pltpu.SemaphoreType.DMA((2, N)),
             pltpu.SemaphoreType.DMA((HALF,)),
             pltpu.SemaphoreType.DMA((HALF,)),
-            pltpu.SemaphoreType.DMA((3, 2, N)),
-            pltpu.SemaphoreType.DMA((3, HEADS)),
+            pltpu.SemaphoreType.DMA((2, 2, N)),
+            pltpu.SemaphoreType.DMA((2, HEADS)),
         ],
         compiler_params=pltpu.CompilerParams(
             collective_id=0, has_side_effects=True, vmem_limit_bytes=60 * 1024 * 1024
@@ -428,7 +443,7 @@
     results = pl.pallas_call(
         hand_on,
         out_shape=(whole, whole, whole),
-        in_specs=[pl.BlockSpec(memory_space=pltpu.VMEM)] * 3,
+        in_specs=[pl.BlockSpec(memory_space=pltpu.VMEM)] * 2,
         out_specs=[pl.BlockSpec(memory_space=pl.ANY)] * 3,
         scratch_shapes=[pltpu.SemaphoreType.DMA((3,))],
         compiler_params=pltpu.CompilerParams(vmem_limit_bytes=8 * 1024 * 1024),

time: 118 us -> 116 us (0.983)
  Pallas kernels: 117 us -> 115 us
    pallas_call x1, Pallas kernels: 115 us -> 114 us  [body(): pl.pallas_call(kernel, out_shape=(pltpu.VMEM((HEADS, ROWS, WIDTH), jnp.bf...]
where the time goes in v8:
time: 116 us
  Pallas kernels  115 us (99%)
    pallas_call x1, Pallas kernels, body(): pl.pallas_call(kernel, out_shape=(pltpu.VMEM((HEADS, ROWS, WIDTH), jnp.bf...  114 us

profile of v8, /device:TPU:1, one launch (start us, length us, event | category | flops | bytes accessed | tf_op | source)
XLA Modules:
  0.0 115.6 jit_solution(12899105435772047442)
XLA Ops:
  0.6 113.6 %attention_backward.1 = (bf16[20,128,128]{2,1,0:T(8,128)(2,1)S(1)}, bf16[20,2,128,128]{3,2,1,0:T(8,128)(2,1)S(1)}) custom-call(bf16[20,128,128]{2,1,0:T(8,128)(2,1)} %bitcast.9, bf16[20,128,128]{2,1,0:T(8,128)(2,1)} %bitcast.10, bf16[20,128,128]{2,1,0:T(8,128)(2,1)} %bitcast.11, bf16[20,128,128]{2,1,0:T(8,128)(2,1)} %bitcast.12, ...), custom_call_target="tpu_custom_call" | custom-call | tf_op jit(solution)/shard_map/attention_backward/pallas_call | solution.py:409
  114.3 1.3 %hand_on.1 = (bf16[20,128,128]{2,1,0:T(8,128)(2,1)}, bf16[20,128,128]{2,1,0:T(8,128)(2,1)}, bf16[20,128,128]{2,1,0:T(8,128)(2,1)}) custom-call(bf16[20,128,128]{2,1,0:T(8,128)(2,1)S(1)} %get-tuple-element.8.dq_ref, bf16[20,2,128,128]{3,2,1,0:T(8,128)(2,1)S(1)} %get-tuple-element.9.dkv_ref), custom_call_target="tpu_custom_call" | custom-call | tf_op jit(solution)/shard_map/hand_on/pallas_call | solution.py:443

commit v9 on v8

--- a/solution.py
+++ b/solution.py
@@ -14,6 +14,7 @@
 EXTRA = HEADS - N
 CHIPS = N // 2
 HALF = CHIPS // 2
+TILE = 4
 PAIR = 2 * ROWS
 LOG2E = math.log2(math.e)
 SCALE = 1.0 / math.sqrt(WIDTH)
@@ -112,6 +113,15 @@
             for kind in kinds:
                 send(kind, dest, 1, dest)
 
+    barrier = pltpu.get_barrier_semaphore()
+
+    def greet(i, carry):
+        pl.semaphore_signal(
+            barrier, inc=1, device_id={"ctx": (me + i) % N}, device_id_type=pl.DeviceIdType.MESH
+        )
+        return carry
+
+    lax.fori_loop(1, N, greet, 0)
     loads = [
         pltpu.make_async_copy(src, dst, load_sem.at[i])
         for i, (src, dst) in enumerate(
@@ -126,15 +136,6 @@
     ]
     for load in loads:
         load.start()
-    barrier = pltpu.get_barrier_semaphore()
-
-    def greet(i, carry):
-        pl.semaphore_signal(
-            barrier, inc=1, device_id={"ctx": (me + i) % N}, device_id_type=pl.DeviceIdType.MESH
-        )
-        return carry
-
-    lax.fori_loop(1, N, greet, 0)
     pl.semaphore_wait(barrier, N - 1)
 
     loads[0].wait()
@@ -147,13 +148,13 @@
     loads[2].wait()
     norm = ln_ref[...].astype(jnp.float32) * LOG2E
     ones = jnp.ones((8, WIDTH), jnp.bfloat16)
-    upper = lax.broadcasted_iota(jnp.int32, (8, ROWS), 0) < 4
+    first = lax.broadcasted_iota(jnp.int32, (2, ROWS), 0) == 0
     for h in range(HEADS):
         product = qg[h, 1].astype(jnp.float32) * ov[h].astype(jnp.float32)
         high = product.astype(jnp.bfloat16)
         low = (product - high.astype(jnp.float32)).astype(jnp.bfloat16)
         delta = (mm_nt(ones, high) + mm_nt(ones, low)).astype(jnp.bfloat16).astype(jnp.float32)
-        auxs[h] = jnp.where(upper, norm[h : h + 1, :], delta)
+        auxs[h] = jnp.where(first, norm[h : h + 1, :], delta[:2])
     for i in range(EXTRA):
         send_extra((AUX,), i)
     send_own_chip((AUX,))
@@ -275,29 +276,36 @@
         keys_t = keys.T
         dk = jnp.zeros((PAIR, WIDTH), jnp.float32)
         dv = jnp.zeros((PAIR, WIDTH), jnp.float32)
-        for t in range(CHIPS):
-            spot = slice(2 * t, 2 * t + 2)
-            queries = qgb[slot, spot, 0].reshape(PAIR, WIDTH)
-            grads = qgb[slot, spot, 1].reshape(PAIR, WIDTH)
-            norms = [auxb[slot, 2 * t + b, 0:1, :] for b in range(2)]
-            delta = jnp.concatenate([auxb[slot, 2 * t + b, 4:5, :] for b in range(2)], axis=1)
-            diagonal = tri[jnp.where(c == t, 1, 0)]
-            scores = mm(keys, qt[t]) * (SCALE * LOG2E)
-            grad_weights = mm(vals, gt[t])
+        for t in range(0, N, TILE):
+            spot = slice(t, t + TILE)
+            queries = qgb[slot, spot, 0].reshape(TILE * ROWS, WIDTH)
+            grads = qgb[slot, spot, 1].reshape(TILE * ROWS, WIDTH)
+            chips = range(t // 2, (t + TILE) // 2)
+            norms = [auxb[slot, t + b, 0:1, :] for b in range(TILE)]
+            delta = jnp.concatenate([auxb[slot, t + b, 1:2, :] for b in range(TILE)], axis=1)
+            diagonal = [tri[jnp.where(c == u, 1, 0)] for u in chips]
+            scores = mm(keys, jnp.concatenate([qt[u] for u in chips], axis=1)) * (SCALE * LOG2E)
+            grad_weights = mm(vals, jnp.concatenate([gt[u] for u in chips], axis=1))
             parts = []
             for kblock in range(2):
                 bias = []
-                for qblock in range(2):
-                    later = pos_ref[2 * c + kblock] > pos_ref[2 * t + qblock]
-                    row = norms[qblock] + jnp.where(later, HIDE, 0.0)
-                    bias.append(row + diagonal if kblock == qblock else jnp.broadcast_to(row, (ROWS, ROWS)))
+                for b in range(TILE):
+                    later = pos_ref[2 * c + kblock] > pos_ref[t + b]
+                    row = norms[b] + jnp.where(later, HIDE, 0.0)
+                    bias.append(
+                        row + diagonal[b // 2]
+                        if kblock == b % 2
+                        else jnp.broadcast_to(row, (ROWS, ROWS))
+                    )
                 part = scores[kblock * ROWS : (kblock + 1) * ROWS]
                 parts.append(jnp.exp2(part - jnp.concatenate(bias, axis=1)))
             weights = jnp.concatenate(parts, axis=0)
             grad_scores = (weights * (grad_weights - delta)).astype(jnp.bfloat16)
             dv += mm(weights.astype(jnp.bfloat16), grads)
             dk += mm(grad_scores, queries)
-            dqa[t] += mm(keys_t, grad_scores)
+            dq = mm(keys_t, grad_scores)
+            for i, u in enumerate(chips):
+                dqa[u] += dq[:, i * PAIR : (i + 1) * PAIR]
         dkvo[slot, pair, 0] = (dk * SCALE).astype(jnp.bfloat16).reshape(2, ROWS, WIDTH)
         dkvo[slot, pair, 1] = dv.astype(jnp.bfloat16).reshape(2, ROWS, WIDTH)
         for b in range(2):
@@ -414,9 +422,9 @@
         out_specs=[pl.BlockSpec(memory_space=pltpu.VMEM)] * 2,
         scratch_shapes=[
             doubles, doubles,
-            pltpu.VMEM((HEADS, 8, ROWS), jnp.float32),
+            pltpu.VMEM((HEADS, 2, ROWS), jnp.float32),
             double_blocks, double_blocks,
-            pltpu.VMEM((2, N, 8, ROWS), jnp.float32),
+            pltpu.VMEM((2, N, 2, ROWS), jnp.float32),
             pltpu.VMEM((HEADS, ROWS, WIDTH), jnp.bfloat16),
             pltpu.VMEM((CHIPS, WIDTH, PAIR), jnp.bfloat16),
             pltpu.VMEM((CHIPS, WIDTH, PAIR), jnp.bfloat16),

time: 116 us -> 114 us (0.983)
    pallas_call x1, Pallas kernels: 114 us -> 112 us  [body(): pl.pallas_call(kernel, out_shape=(pltpu.VMEM((HEADS, ROWS, WIDTH), jnp.bf...]
where the time goes in v9:
time: 114 us
  Pallas kernels  114 us (100%)
    pallas_call x1, Pallas kernels, body(): pl.pallas_call(kernel, out_shape=(pltpu.VMEM((HEADS, ROWS, WIDTH), jnp.bf...  112 us

profile of v9, /device:TPU:1, one launch (start us, length us, event | category | flops | bytes accessed | tf_op | source)
XLA Modules:
  0.0 114.3 jit_solution(12592830207598207661)
XLA Ops:
  0.6 112.4 %attention_backward.1 = (bf16[20,128,128]{2,1,0:T(8,128)(2,1)S(1)}, bf16[20,2,128,128]{3,2,1,0:T(8,128)(2,1)S(1)}) custom-call(bf16[20,128,128]{2,1,0:T(8,128)(2,1)} %bitcast.9, bf16[20,128,128]{2,1,0:T(8,128)(2,1)} %bitcast.10, bf16[20,128,128]{2,1,0:T(8,128)(2,1)} %bitcast.11, bf16[20,128,128]{2,1,0:T(8,128)(2,1)} %bitcast.12, ...), custom_call_target="tpu_custom_call" | custom-call | tf_op jit(solution)/shard_map/attention_backward/pallas_call | solution.py:417
  113.0 1.3 %hand_on.1 = (bf16[20,128,128]{2,1,0:T(8,128)(2,1)}, bf16[20,128,128]{2,1,0:T(8,128)(2,1)}, bf16[20,128,128]{2,1,0:T(8,128)(2,1)}) custom-call(bf16[20,128,128]{2,1,0:T(8,128)(2,1)S(1)} %get-tuple-element.8.dq_ref, bf16[20,2,128,128]{3,2,1,0:T(8,128)(2,1)S(1)} %get-tuple-element.9.dkv_ref), custom_call_target="tpu_custom_call" | custom-call | tf_op jit(solution)/shard_map/hand_on/pallas_call | solution.py:451

commit v10 on v9

--- a/solution.py
+++ b/solution.py
@@ -23,13 +23,13 @@
 DQ, DKV = range(2)
 
 
-FAR_AND_NEAR = (4, 1, 5, 2, 7, 3, 6)
-
-
-def arrival(step):
+FAR_TO_NEAR = (4, 3, 5, 2, 6, 1, 7)
+
+
+def sent_at(step):
     offset = 0
-    for i, sent in enumerate(FAR_AND_NEAR):
-        offset = jnp.where(step == i + 1, CHIPS - sent, offset)
+    for i, sent in enumerate(FAR_TO_NEAR):
+        offset = jnp.where(step == i + 1, sent, offset)
     return offset
 
 
@@ -50,6 +50,7 @@
     me = lax.axis_index("ctx")
     chip = me // 2
     core = me % 2
+    sign = 1 - 2 * core
     shares = core == 0
     toward = 2 * (chip % 2) - 1
     partner = me - 2 * toward
@@ -109,7 +110,7 @@
 
     def send_main(kinds, i):
         for b in range(2):
-            dest = 2 * ((chip + FAR_AND_NEAR[i]) % CHIPS) + (core + b) % 2
+            dest = 2 * ((chip + sign * FAR_TO_NEAR[i] + CHIPS) % CHIPS) + (core + b) % 2
             for kind in kinds:
                 send(kind, dest, 1, dest)
 
@@ -218,7 +219,7 @@
             pltpu.make_async_copy(src, dst, out_recv.at[kind, head]).start()
 
     def around(i):
-        return (chip + arrival(i)) % CHIPS
+        return (chip - sign * sent_at(i) + CHIPS) % CHIPS
 
     def pass_part(i):
         return pltpu.make_async_remote_copy(
@@ -337,7 +338,7 @@
         @pl.when(step == HALF + CHIPS - 1)
         def _():
             def finish(i, carry):
-                c = around(i)
+                c = around((i + 1) % CHIPS)
                 done = (dqa[c] * SCALE).T.astype(jnp.bfloat16)
                 dqo[1, pl.ds(2 * c, 2)] = done.reshape(2, ROWS, WIDTH)
                 for b in range(2):

time: 114 us -> 115 us (level)
  no operation moved by 1% of the time
where the time goes in v10:
time: 115 us
  Pallas kernels  114 us (99%)
    pallas_call x1, Pallas kernels, body(): pl.pallas_call(kernel, out_shape=(pltpu.VMEM((HEADS, ROWS, WIDTH), jnp.bf...  113 us

profile of v10, /device:TPU:1, one launch (start us, length us, event | category | flops | bytes accessed | tf_op | source)
XLA Modules:
  0.0 114.5 jit_solution(6567716987679973712)
XLA Ops:
  0.6 112.6 %attention_backward.1 = (bf16[20,128,128]{2,1,0:T(8,128)(2,1)S(1)}, bf16[20,2,128,128]{3,2,1,0:T(8,128)(2,1)S(1)}) custom-call(bf16[20,128,128]{2,1,0:T(8,128)(2,1)} %bitcast.9, bf16[20,128,128]{2,1,0:T(8,128)(2,1)} %bitcast.10, bf16[20,128,128]{2,1,0:T(8,128)(2,1)} %bitcast.11, bf16[20,128,128]{2,1,0:T(8,128)(2,1)} %bitcast.12, ...), custom_call_target="tpu_custom_call" | custom-call | tf_op jit(solution)/shard_map/attention_backward/pallas_call | solution.py:418
  113.2 1.3 %hand_on.1 = (bf16[20,128,128]{2,1,0:T(8,128)(2,1)}, bf16[20,128,128]{2,1,0:T(8,128)(2,1)}, bf16[20,128,128]{2,1,0:T(8,128)(2,1)}) custom-call(bf16[20,128,128]{2,1,0:T(8,128)(2,1)S(1)} %get-tuple-element.8.dq_ref, bf16[20,2,128,128]{3,2,1,0:T(8,128)(2,1)S(1)} %get-tuple-element.9.dkv_ref), custom_call_target="tpu_custom_call" | custom-call | tf_op jit(solution)/shard_map/hand_on/pallas_call | solution.py:452

commit v11 on v10

--- a/solution.py
+++ b/solution.py
@@ -31,6 +31,25 @@
     for i, sent in enumerate(FAR_TO_NEAR):
         offset = jnp.where(step == i + 1, sent, offset)
     return offset
+
+
+LAST_ORDERS = (
+    (4, 3, 2, 5, 1, 0, 6, 7),
+    (5, 4, 3, 0, 2, 1, 6, 7),
+    (6, 7, 0, 3, 1, 2, 5, 4),
+    (7, 0, 6, 1, 2, 3, 5, 4),
+    (0, 1, 7, 2, 3, 6, 4, 5),
+    (1, 0, 2, 3, 7, 5, 4, 6),
+    (2, 3, 1, 0, 4, 6, 7, 5),
+    (3, 2, 1, 0, 4, 7, 5, 6),
+)
+
+
+def last_order(chip):
+    code = 0
+    for i, order in enumerate(LAST_ORDERS):
+        code = jnp.where(chip == i, sum(c * 8**j for j, c in enumerate(order)), code)
+    return code
 
 
 def mm(a, b):
@@ -337,15 +356,15 @@
 
         @pl.when(step == HALF + CHIPS - 1)
         def _():
-            def finish(i, carry):
-                c = around((i + 1) % CHIPS)
+            def finish(i, orders):
+                c = orders % 8
                 done = (dqa[c] * SCALE).T.astype(jnp.bfloat16)
                 dqo[1, pl.ds(2 * c, 2)] = done.reshape(2, ROWS, WIDTH)
                 for b in range(2):
                     give(DQ, 1, me, 2 * c + b)
-                return carry
-
-            lax.fori_loop(0, CHIPS, finish, 0)
+                return orders // 8
+
+            lax.fori_loop(0, CHIPS, finish, last_order(chip))
 
         return carry
 

time: 115 us -> 115 us (level)
  no operation moved by 1% of the time
where the time goes in v11:
time: 115 us
  Pallas kernels  114 us (99%)
    pallas_call x1, Pallas kernels, body(): pl.pallas_call(kernel, out_shape=(pltpu.VMEM((HEADS, ROWS, WIDTH), jnp.bf...  113 us

profile of v11, /device:TPU:1, one launch (start us, length us, event | category | flops | bytes accessed | tf_op | source)
XLA Modules:
  0.0 114.5 jit_solution(3383624314347605993)
XLA Ops:
  0.6 112.6 %attention_backward.1 = (bf16[20,128,128]{2,1,0:T(8,128)(2,1)S(1)}, bf16[20,2,128,128]{3,2,1,0:T(8,128)(2,1)S(1)}) custom-call(bf16[20,128,128]{2,1,0:T(8,128)(2,1)} %bitcast.9, bf16[20,128,128]{2,1,0:T(8,128)(2,1)} %bitcast.10, bf16[20,128,128]{2,1,0:T(8,128)(2,1)} %bitcast.11, bf16[20,128,128]{2,1,0:T(8,128)(2,1)} %bitcast.12, ...), custom_call_target="tpu_custom_call" | custom-call | tf_op jit(solution)/shard_map/attention_backward/pallas_call | solution.py:437
  113.2 1.3 %hand_on.1 = (bf16[20,128,128]{2,1,0:T(8,128)(2,1)}, bf16[20,128,128]{2,1,0:T(8,128)(2,1)}, bf16[20,128,128]{2,1,0:T(8,128)(2,1)}) custom-call(bf16[20,128,128]{2,1,0:T(8,128)(2,1)S(1)} %get-tuple-element.8.dq_ref, bf16[20,2,128,128]{3,2,1,0:T(8,128)(2,1)S(1)} %get-tuple-element.9.dkv_ref), custom_call_target="tpu_custom_call" | custom-call | tf_op jit(solution)/shard_map/hand_on/pallas_call | solution.py:471

commit v12 on v10

--- a/solution.py
+++ b/solution.py
@@ -77,7 +77,7 @@
         pltpu.make_async_remote_copy(
             src_ref=sources[kind].at[head],
             dst_ref=landing[kind].at[slot, me],
-            send_sem=in_send.at[kind, head],
+            send_sem=in_send.at[kind],
             recv_sem=in_recv.at[kind, slot, me],
             device_id={"ctx": dest},
             device_id_type=pl.DeviceIdType.MESH,
@@ -180,7 +180,7 @@
                     pltpu.make_async_remote_copy(
                         src_ref=landing[kind].at[0, block],
                         dst_ref=landing[kind].at[0, block],
-                        send_sem=fwd_send.at[kind - QG, block],
+                        send_sem=fwd_send.at[kind - QG],
                         recv_sem=in_recv.at[kind, 0, block],
                         device_id={"ctx": partner},
                         device_id_type=pl.DeviceIdType.MESH,
@@ -208,15 +208,15 @@
             pltpu.make_async_remote_copy(
                 src_ref=src,
                 dst_ref=dst,
-                send_sem=out_send.at[kind, slot, dest],
-                recv_sem=out_recv.at[kind, head],
+                send_sem=out_send.at[kind, slot],
+                recv_sem=out_recv.at[kind],
                 device_id={"ctx": dest},
                 device_id_type=pl.DeviceIdType.MESH,
             ).start()
 
         @pl.when(dest == me)
         def _():
-            pltpu.make_async_copy(src, dst, out_recv.at[kind, head]).start()
+            pltpu.make_async_copy(src, dst, out_recv.at[kind]).start()
 
     def around(i):
         return (chip - sign * sent_at(i) + CHIPS) % CHIPS
@@ -225,7 +225,7 @@
         return pltpu.make_async_remote_copy(
             src_ref=part_out.at[i],
             dst_ref=part_in.at[i],
-            send_sem=part_send.at[i],
+            send_sem=part_send.at[0],
             recv_sem=part_recv.at[i],
             device_id={"ctx": partner},
             device_id_type=pl.DeviceIdType.MESH,
@@ -351,49 +351,24 @@
 
     lax.fori_loop(jnp.where(shares, 0, HALF), HALF + CHIPS, one_pair, 0)
 
-    def drain_in(h, carry):
-        owner = jnp.where(h < N, h, nearer(jnp.maximum(h - N, 0)))
-
-        @pl.when(owner != me)
-        def _():
-            for kind in range(3):
-                wait(sources[kind].at[h], in_send.at[kind, h])
-
-        return carry
-
-    lax.fori_loop(0, HEADS, drain_in, 0)
-
-    def drain_out(slot, dest):
-        @pl.when(dest != me)
-        def _():
-            for kind in range(2):
-                wait(staged[kind].at[slot, dest], out_send.at[kind, slot, dest])
-
-    def drain_main(dest, carry):
-        drain_out(1, dest)
-        return carry
-
-    lax.fori_loop(0, N, drain_main, 0)
-
     @pl.when(shares)
     def _():
-        def drain_shared(i, carry):
-            pass_part(i).wait_send()
-            for b in range(2):
-                block = 2 * near(i) + b
-                drain_out(0, block)
-                for kind in (AUX, QG):
-                    wait(landing[kind].at[0, block], fwd_send.at[kind - QG, block])
-            return carry
-
-        lax.fori_loop(0, HALF, drain_shared, 0)
-
-    def collect(h, carry):
+        for kind in range(3):
+            wait(sources[kind].at[pl.ds(0, HEADS - 2)], in_send.at[kind])
+        for kind in (AUX, QG):
+            wait(landing[kind].at[0, pl.ds(0, CHIPS)], fwd_send.at[kind - QG])
+        wait(part_out, part_send.at[0])
         for kind in range(2):
-            wait(results[kind].at[h], out_recv.at[kind, h])
-        return carry
-
-    lax.fori_loop(0, HEADS, collect, 0)
+            wait(staged[kind].at[0, pl.ds(0, CHIPS - 1)], out_send.at[kind, 0])
+
+    @pl.when(jnp.logical_not(shares))
+    def _():
+        for kind in range(3):
+            wait(sources[kind].at[pl.ds(0, HEADS - 1)], in_send.at[kind])
+
+    for kind in (DKV, DQ):
+        wait(staged[kind].at[1, pl.ds(0, N - 1)], out_send.at[kind, 1])
+        wait(results[kind], out_recv.at[kind])
 
 
 def hand_on(dq_ref, dkv_ref, dq_out, dk_out, dv_out, sem):
@@ -436,13 +411,13 @@
             pltpu.VMEM((HALF, PAIR, WIDTH), jnp.bfloat16),
             pltpu.VMEM((HALF, PAIR, WIDTH), jnp.bfloat16),
             pltpu.SemaphoreType.DMA((5,)),
-            pltpu.SemaphoreType.DMA((3, HEADS)),
+            pltpu.SemaphoreType.DMA((3,)),
             pltpu.SemaphoreType.DMA((3, 2, N)),
-            pltpu.SemaphoreType.DMA((2, N)),
+            pltpu.SemaphoreType.DMA((2,)),
+            pltpu.SemaphoreType.DMA((1,)),
             pltpu.SemaphoreType.DMA((HALF,)),
-            pltpu.SemaphoreType.DMA((HALF,)),
-            pltpu.SemaphoreType.DMA((2, 2, N)),
-            pltpu.SemaphoreType.DMA((2, HEADS)),
+            pltpu.SemaphoreType.DMA((2, 2)),
+            pltpu.SemaphoreType.DMA((2,)),
         ],
         compiler_params=pltpu.CompilerParams(
             collective_id=0, has_side_effects=True, vmem_limit_bytes=60 * 1024 * 1024

time: 115 us -> 113 us (0.983)
  Pallas kernels: 114 us -> 112 us
    pallas_call x1, Pallas kernels: 113 us -> 111 us  [body(): pl.pallas_call(kernel, out_shape=(pltpu.VMEM((HEADS, ROWS, WIDTH), jnp.bf...]
where the time goes in v12:
time: 113 us
  Pallas kernels  112 us (99%)
    pallas_call x1, Pallas kernels, body(): pl.pallas_call(kernel, out_shape=(pltpu.VMEM((HEADS, ROWS, WIDTH), jnp.bf...  111 us

profile of v12, /device:TPU:1, one launch (start us, length us, event | category | flops | bytes accessed | tf_op | source)
XLA Modules:
  0.0 112.7 jit_solution(4300946431387904535)
XLA Ops:
  0.6 110.8 %attention_backward.1 = (bf16[20,128,128]{2,1,0:T(8,128)(2,1)S(1)}, bf16[20,2,128,128]{3,2,1,0:T(8,128)(2,1)S(1)}) custom-call(bf16[20,128,128]{2,1,0:T(8,128)(2,1)} %bitcast.9, bf16[20,128,128]{2,1,0:T(8,128)(2,1)} %bitcast.10, bf16[20,128,128]{2,1,0:T(8,128)(2,1)} %bitcast.11, bf16[20,128,128]{2,1,0:T(8,128)(2,1)} %bitcast.12, ...), custom_call_target="tpu_custom_call" | custom-call | tf_op jit(solution)/shard_map/attention_backward/pallas_call | solution.py:393
  111.4 1.3 %hand_on.1 = (bf16[20,128,128]{2,1,0:T(8,128)(2,1)}, bf16[20,128,128]{2,1,0:T(8,128)(2,1)}, bf16[20,128,128]{2,1,0:T(8,128)(2,1)}) custom-call(bf16[20,128,128]{2,1,0:T(8,128)(2,1)S(1)} %get-tuple-element.8.dq_ref, bf16[20,2,128,128]{3,2,1,0:T(8,128)(2,1)S(1)} %get-tuple-element.9.dkv_ref), custom_call_target="tpu_custom_call" | custom-call | tf_op jit(solution)/shard_map/hand_on/pallas_call | solution.py:427

commit v13 on v12

--- a/solution.py
+++ b/solution.py
@@ -78,14 +78,14 @@
             src_ref=sources[kind].at[head],
             dst_ref=landing[kind].at[slot, me],
             send_sem=in_send.at[kind],
-            recv_sem=in_recv.at[kind, slot, me],
+            recv_sem=in_recv.at[kind, slot, chip],
             device_id={"ctx": dest},
             device_id_type=pl.DeviceIdType.MESH,
         ).start()
 
     def keep(kind, head, slot):
         pltpu.make_async_copy(
-            sources[kind].at[head], landing[kind].at[slot, me], in_recv.at[kind, slot, me]
+            sources[kind].at[head], landing[kind].at[slot, me], in_recv.at[kind, slot, chip]
         ).start()
 
     def send_extra(kinds, i):
@@ -141,10 +141,10 @@
 
     loads[0].wait()
     loads[1].wait()
-    send_own_chip((QG,))
     for i in range(2):
         send_main((QG,), i)
         send_extra((QG,), i)
+    send_own_chip((QG,))
 
     loads[2].wait()
     norm = ln_ref[...].astype(jnp.float32) * LOG2E
@@ -173,18 +173,17 @@
     @pl.when(shares)
     def _():
         def forward(i, carry):
-            for b in range(2):
-                block = 2 * near(i) + b
-                for kind in (AUX, QG):
-                    wait(landing[kind].at[0, block], in_recv.at[kind, 0, block])
-                    pltpu.make_async_remote_copy(
-                        src_ref=landing[kind].at[0, block],
-                        dst_ref=landing[kind].at[0, block],
-                        send_sem=fwd_send.at[kind - QG],
-                        recv_sem=in_recv.at[kind, 0, block],
-                        device_id={"ctx": partner},
-                        device_id_type=pl.DeviceIdType.MESH,
-                    ).start()
+            pair = pl.ds(2 * near(i), 2)
+            for kind in (AUX, QG):
+                wait(landing[kind].at[0, pair], in_recv.at[kind, 0, near(i)])
+                pltpu.make_async_remote_copy(
+                    src_ref=landing[kind].at[0, pair],
+                    dst_ref=landing[kind].at[0, pair],
+                    send_sem=fwd_send.at[kind - QG],
+                    recv_sem=in_recv.at[kind, 0, near(i)],
+                    device_id={"ctx": partner},
+                    device_id_type=pl.DeviceIdType.MESH,
+                ).start()
             return carry
 
         lax.fori_loop(0, HALF, forward, 0)
@@ -236,9 +235,8 @@
         gt[c] = qgb[slot, pl.ds(2 * c, 2), 1].reshape(PAIR, WIDTH).T
 
     def queries_arrived(slot, c):
-        for b in range(2):
-            for kind in (AUX, QG):
-                wait(landing[kind].at[slot, 2 * c + b], in_recv.at[kind, slot, 2 * c + b])
+        for kind in (AUX, QG):
+            wait(landing[kind].at[slot, pl.ds(2 * c, 2)], in_recv.at[kind, slot, c])
         turned(slot, c)
 
     def one_pair(step, carry):
@@ -268,9 +266,7 @@
             lax.fori_loop(0, CHIPS, ready, 0)
 
         c = jnp.where(slot == 0, near(turn), around(turn))
-        for b in range(2):
-            for kind in (KV,):
-                wait(landing[kind].at[slot, 2 * c + b], in_recv.at[kind, slot, 2 * c + b])
+        wait(landing[KV].at[slot, pl.ds(2 * c, 2)], in_recv.at[KV, slot, c])
         pair = pl.ds(2 * c, 2)
         keys = kvb[slot, pair, 0].reshape(PAIR, WIDTH)
         vals = kvb[slot, pair, 1].reshape(PAIR, WIDTH)
@@ -412,7 +408,7 @@
             pltpu.VMEM((HALF, PAIR, WIDTH), jnp.bfloat16),
             pltpu.SemaphoreType.DMA((5,)),
             pltpu.SemaphoreType.DMA((3,)),
-            pltpu.SemaphoreType.DMA((3, 2, N)),
+            pltpu.SemaphoreType.DMA((3, 2, CHIPS)),
             pltpu.SemaphoreType.DMA((2,)),
             pltpu.SemaphoreType.DMA((1,)),
             pltpu.SemaphoreType.DMA((HALF,)),

time: 113 us -> 112 us (level)
  no operation moved by 1% of the time
where the time goes in v13:
time: 112 us
  Pallas kernels  112 us (100%)
    pallas_call x1, Pallas kernels, body(): pl.pallas_call(kernel, out_shape=(pltpu.VMEM((HEADS, ROWS, WIDTH), jnp.bf...  110 us

profile of v13, /device:TPU:1, one launch (start us, length us, event | category | flops | bytes accessed | tf_op | source)
XLA Modules:
  0.0 112.2 jit_solution(4453505293563974206)
XLA Ops:
  0.6 110.3 %attention_backward.1 = (bf16[20,128,128]{2,1,0:T(8,128)(2,1)S(1)}, bf16[20,2,128,128]{3,2,1,0:T(8,128)(2,1)S(1)}) custom-call(bf16[20,128,128]{2,1,0:T(8,128)(2,1)} %bitcast.9, bf16[20,128,128]{2,1,0:T(8,128)(2,1)} %bitcast.10, bf16[20,128,128]{2,1,0:T(8,128)(2,1)} %bitcast.11, bf16[20,128,128]{2,1,0:T(8,128)(2,1)} %bitcast.12, ...), custom_call_target="tpu_custom_call" | custom-call | tf_op jit(solution)/shard_map/attention_backward/pallas_call | solution.py:389
  110.9 1.3 %hand_on.1 = (bf16[20,128,128]{2,1,0:T(8,128)(2,1)}, bf16[20,128,128]{2,1,0:T(8,128)(2,1)}, bf16[20,128,128]{2,1,0:T(8,128)(2,1)}) custom-call(bf16[20,128,128]{2,1,0:T(8,128)(2,1)S(1)} %get-tuple-element.8.dq_ref, bf16[20,2,128,128]{3,2,1,0:T(8,128)(2,1)S(1)} %get-tuple-element.9.dkv_ref), custom_call_target="tpu_custom_call" | custom-call | tf_op jit(solution)/shard_map/hand_on/pallas_call | solution.py:423
